TPU v7x, 32 devices: a whole 2x2x4 slice. The times are simulated.
32 devices in a mesh: ctx: 4 (over y, x), head: 8 (over z, core).
Axes of the slice: x: 2, y: 2, z: 4, core: 2. Of those that a mesh axis runs over, the one named last changes fastest.
Arguments:
- queries: bfloat16 [2, 2048, 2048], P(None, 'ctx', 'head'), may hold values from -6 to 6
- keys: bfloat16 [2, 2048, 2048], P(None, 'ctx', 'head'), may hold values from -6 to 6
- values: bfloat16 [2, 2048, 2048], P(None, 'ctx', 'head'), may hold values from -6 to 6
- rates: float32 [8, 2, 2048], P('head', None, 'ctx'), may hold values from 0.05 to 1
- w_gate: float32 [8, 256, 512], P('head'), may hold values from -0.375 to 0.375
- w_up: float32 [8, 256, 512], P('head'), may hold values from -0.375 to 0.375
- w_down: float32 [8, 512, 256], P('head'), may hold values from -0.25 to 0.25
- gains: float32 [8, 256], P('head'), may hold values from 0.25 to 0.6
- out_proj: bfloat16 [2048, 2048], P('head'), may hold values from -0.1875 to 0.1875
Outputs:
- output: bfloat16 [2, 2048, 2048], P(None, 'ctx', 'head')
All inputs are finite; a program needn't handle non-finite values.
Results may differ from a plain program's by a relative error of at most 0.0051.
Values may be sent and summed in bfloat16 or wider, within the bound.
No kernel may reach another device: no remote copies, remote signals or barrier semaphores. Data moves between devices by JAX's collectives and lax.ppermute only.
A program may use at most 128 MiB of HBM per device.

v0:
```python
import functools

import jax
import jax.numpy as jnp
from jax import lax
from jax.experimental import pallas as pl
from jax.experimental.pallas import tpu as pltpu
from jax.sharding import PartitionSpec as P

WINDOW = 256
NS_ITERS = 5
RATE_ROWS = 16
VMEM_LIMIT = 20 * 1024 * 1024
PIECES = 8
UPDATE_FLOPS = 30_000_000_000
MESSAGE_VMEM = 60 * 1024 * 1024

attn_temp = 5.0
step_size = 0.5
quintic_one = 3.4445
quintic_two = -4.775
quintic_three = 2.0315

f32 = jnp.float32
bf16 = jnp.bfloat16
NN = (((1,), (0,)), ((), ()))
NT = (((1,), (1,)), ((), ()))


def mm(left, right, dims=NN):
    return lax.dot_general(left, right, dims, preferred_element_type=f32)


def split(value):
    high = value.astype(bf16)
    return high, (value - high.astype(f32)).astype(bf16)


def cat(parts, axis):
    return jnp.concatenate(parts, axis=axis)


def mm_split(left, right):
    return mm(cat([left[0], left[0], left[1]], 1), cat([right[0], right[1], right[0]], 0))


def unit_scale(rows):
    wide = rows.astype(f32)
    return lax.rsqrt(jnp.sum(wide * wide, axis=-1, keepdims=True) + 1e-06)


def silu_parts(gate_pre):
    sigma = 0.5 * jnp.tanh(0.5 * gate_pre) + 0.5
    return sigma, gate_pre * sigma


def rate_column(packed, token_blocks):
    turned = packed.astype(f32).T
    columns = []
    for at in range(token_blocks):
        parts = [turned[:, at + token_blocks * piece : at + token_blocks * piece + 1] for piece in range(3)]
        columns.append(parts[0] + parts[1] + parts[2])
    return cat(columns, 0)


def stacked_split(value):
    return cat(split(value), 0)


def joined(stacked):
    rows = stacked.shape[0] // 2
    return stacked[:rows].astype(f32) + stacked[rows:].astype(f32)


TOKEN_TILE = 256


def add_chunk(acc, key_ref, value_ref, rate_ref, gate_up_ref, down_turned_ref):
    hidden_width = down_turned_ref.shape[1]
    tiles = value_ref.shape[0] // TOKEN_TILE
    rate = rate_column(rate_ref[...], tiles)
    state = [{} for _ in range(tiles)]

    def forward(at):
        tile = state[at]
        rows = slice(at * TOKEN_TILE, at * TOKEN_TILE + TOKEN_TILE)
        keys, values = key_ref[rows], value_ref[rows]
        tile["rate"], tile["scale"] = rate[rows], unit_scale(keys)
        tile["keys"], tile["values"] = keys.T, values.T
        tile["pre"] = mm(cat([keys, keys], 1), gate_up_ref[...])
        tile["back"] = mm(cat([values, values], 1), down_turned_ref[...])

    def middle(at):
        tile = state[at]
        pre = tile["pre"] * tile["scale"]
        gate_pre, up_pre = pre[:, :hidden_width], pre[:, hidden_width:]
        sigma, gate_act = silu_parts(gate_pre)
        back = tile["back"] * (tile["rate"] * tile["scale"])
        slope = sigma + gate_act * (1.0 - sigma)
        terms = (back * up_pre * slope, back * gate_act, gate_act * up_pre * tile["rate"])
        tile["terms"] = [cat(split(term), 0) for term in terms]

    def backward(at):
        tile = state[at]
        turned = [cat([tile[name]] * 2, 1) for name in ("keys", "keys", "values")]
        for place, (left, right) in enumerate(zip(turned, tile["terms"])):
            part = mm(left, right)
            acc[place] = part if acc[place] is None else acc[place] + part

    for step in range(tiles + 2):
        for lag, stage in enumerate((forward, middle, backward)):
            if 0 <= step - lag < tiles:
                stage(step - lag)


NS_PASSES = (1, 1, 3, 3, 3)


def parts_of(value, passes):
    return (value.astype(bf16),) if passes == 1 else split(value)


def plus_turned(matrix):
    return matrix + matrix.T


def gram_of(parts):
    whole = mm(parts[0], parts[0], NT)
    return whole if len(parts) == 1 else whole + plus_turned(mm(parts[0], parts[1], NT))


def square_of(parts):
    whole = mm(parts[0], parts[0])
    return whole if len(parts) == 1 else whole + plus_turned(mm(parts[0], parts[1]))


def product_of(left, right):
    return mm(left[0], right[0]) if len(left) == 1 else mm_split(left, right)


def orthogonal(grads):
    iterates = [
        grad * (1.0 / (jnp.sqrt(jnp.sum(grad * grad, keepdims=True)) + 1e-06)) for grad in grads
    ]
    for passes in NS_PASSES:
        parts = [parts_of(iterate, passes) for iterate in iterates]
        grams = [gram_of(part) for part in parts]
        squares = [square_of(parts_of(gram, passes)) for gram in grams]
        polys = [quintic_two * gram + quintic_three * square for gram, square in zip(grams, squares)]
        iterates = [
            quintic_one * iterate + product_of(parts_of(poly, passes), part)
            for iterate, poly, part in zip(iterates, polys, parts)
        ]
    return iterates


def band(query_rows, key_rows, value_rows, masked):
    query_half = (query_rows.astype(f32) * unit_scale(query_rows)).astype(bf16)
    key_half = (key_rows.astype(f32) * unit_scale(key_rows)).astype(bf16)
    scores = mm(query_half, key_half, NT)
    query_pos = lax.broadcasted_iota(jnp.int32, scores.shape, 0)
    key_pos = lax.broadcasted_iota(jnp.int32, scores.shape, 1)
    distance = query_pos + WINDOW - key_pos
    valid = (distance >= 0) & (distance < WINDOW)
    if masked is not None:
        valid = valid & ((key_pos >= WINDOW) | jnp.logical_not(masked))
    weights = jnp.where(valid, jnp.exp(attn_temp * (scores - 1.0)), 0.0)
    probs = (weights / jnp.sum(weights, axis=-1, keepdims=True)).astype(bf16)
    return mm(probs, value_rows)


def apply_fast(query_rows, gate_up, down_turned, gains):
    hidden_width = down_turned.shape[1]
    width = down_turned.shape[0] // 2
    pre = mm(cat([query_rows, query_rows], 1), gate_up) * unit_scale(query_rows)
    gate_pre, up_pre = pre[:, :hidden_width], pre[:, hidden_width:]
    high, low = split(silu_parts(gate_pre)[1] * up_pre)
    down_high, down_low = down_turned[:width], down_turned[width:]
    fast_out = mm(cat([high, high, low], 1), cat([down_high, down_low, down_high], 1), NT)
    mean_square = jnp.mean(fast_out * fast_out, axis=-1, keepdims=True)
    return fast_out * lax.rsqrt(mean_square + 1e-05) * gains


def rate_tile(rates_ref, group, blocks):
    left = [rates_ref[0, group : group + 1, at * 256 : at * 256 + 256] for at in range(blocks)]
    row_at = lax.broadcasted_iota(jnp.int32, (RATE_ROWS, 256), 0)
    tile = jnp.zeros((RATE_ROWS, 256), f32)
    for part in range(3):
        for at in range(blocks):
            rounded = left[at].astype(bf16).astype(f32)
            left[at] = left[at] - rounded
            tile = jnp.where(row_at == part * blocks + at, rounded, tile)
    return tile.astype(bf16)


def message_kernel(group, keys_ref, values_ref, rates_ref, out_ref, sems):
    rows = keys_ref.shape[1]
    piece = 2 * rows // PIECES
    copies = []
    for at in range(PIECES):
        start = at * piece
        source = keys_ref if start < rows else values_ref
        copies.append(pltpu.make_async_copy(
            source.at[group, pl.ds(start % rows, piece)], out_ref.at[pl.ds(start, piece)], sems.at[at]
        ))
        copies[-1].start()
    out_ref[2 * rows :] = rate_tile(rates_ref, group, rows // 256)
    for copy in copies:
        copy.wait()


def later_message_kernel(group, keys_ref, values_ref, rates_ref, out_ref):
    rows = keys_ref.shape[1]
    out_ref[:rows] = keys_ref[group]
    out_ref[rows : 2 * rows] = values_ref[group]
    out_ref[2 * rows :] = rate_tile(rates_ref, group, rows // 256)


def message_parts(message_ref):
    rows = (message_ref.shape[0] - RATE_ROWS) // 2
    return message_ref.at[:rows], message_ref.at[rows : 2 * rows], message_ref.at[2 * rows :]


def local_band_kernel(queries_ref, keys_ref, values_ref, out_ref):
    groups, rows, _ = queries_ref.shape
    for group in range(groups):
        for at in range(1, rows // WINDOW):
            upper = (at + 1) * WINDOW
            out_ref[group, at * WINDOW - WINDOW : at * WINDOW] = band(
                queries_ref[group, at * WINDOW : upper],
                keys_ref[group, upper - 2 * WINDOW : upper],
                values_ref[group, upper - 2 * WINDOW : upper],
                None,
            )


def first_grads_kernel(message, gate_ref, up_ref, down_ref, out_ref, gate_up_ref, down_turned_ref):
    gate_up_ref[...] = stacked_split(cat([gate_ref[...], up_ref[...]], 1))
    down_turned_ref[...] = stacked_split(down_ref[...].T)
    acc = [None] * 3
    add_chunk(acc, *message_parts(message), gate_up_ref, down_turned_ref)
    for at in range(3):
        out_ref[at] = acc[at]


def grads_kernel(chunks, carried, *refs):
    messages, refs = refs[:chunks], refs[chunks:]
    gate_up_ref, down_turned_ref = refs[:2]
    out_ref = refs[-1]
    acc = [refs[2][at] for at in range(3)] if carried else [None] * 3
    for message in messages:
        add_chunk(acc, *message_parts(message), gate_up_ref, down_turned_ref)
    for at in range(3):
        out_ref[at] = acc[at]


def last_grads_kernel(parts, *refs):
    gate_up_ref, down_turned_ref, acc_ref, out_ref, held = refs[parts:]
    start = 0
    for ref in refs[:parts]:
        held[start : start + ref.shape[0]] = ref[...]
        start += ref.shape[0]
    acc = [acc_ref[at] for at in range(3)]
    add_chunk(acc, *message_parts(held), gate_up_ref, down_turned_ref)
    for at in range(3):
        out_ref[at] = acc[at]


def tails(refs, rows):
    found = []
    for end in (rows, 2 * rows):
        for ref in refs:
            if end <= ref.shape[0]:
                found.append(ref[end - WINDOW : end])
                break
            end = end - ref.shape[0]
    return found


def update_kernel(group, counts, *refs):
    near, refs = refs[: counts[0]], refs[counts[0] :]
    last, refs = refs[: counts[1]], refs[counts[1] :]
    past, refs = refs[: counts[2]], refs[counts[2] :]
    gate_up_ref, down_turned_ref, acc_ref, queries_ref, keys_ref, values_ref, local_ref, gains_ref, *refs = refs
    out_ref, gate_up_out, down_turned_out = refs
    ortho = orthogonal([acc_ref[at] for at in range(3)])
    gate_up_out[...] = stacked_split(joined(gate_up_ref) + step_size * cat(ortho[:2], 1))
    down_turned_out[...] = stacked_split(joined(down_turned_ref) + step_size * ortho[2])
    rows = queries_ref.shape[1]
    query_rows = queries_ref.at[group]
    place = lax.axis_index("ctx")
    is_first = place == 0
    is_near = lax.rem(place, 2) == 1
    halo = [jnp.where(is_near, *pair) for pair in zip(tails(near, rows), tails(last, rows))]
    if group > 0:
        halo = [jnp.where(is_first, *pair) for pair in zip(tails(past, rows), halo)]
    head_block = band(
        query_rows[:WINDOW],
        cat([halo[0], keys_ref[group, :WINDOW]], 0),
        cat([halo[1], values_ref[group, :WINDOW]], 0),
        is_first if group == 0 else None,
    )
    normed = apply_fast(query_rows[...], gate_up_out[...], down_turned_out[...], gains_ref[...])
    out_ref[:WINDOW] = (head_block + normed[:WINDOW]).astype(bf16)
    if rows > WINDOW:
        out_ref[WINDOW:] = (local_ref[group] + normed[WINDOW:]).astype(bf16)


def pick_kernel(proj_ref, own_ref, other_ref):
    core = lax.rem(lax.axis_index("head"), 2)
    width = proj_ref.shape[0]
    for chip in range(own_ref.shape[1] // width):
        span = slice(chip * width, chip * width + width)
        for side, ref in ((core, own_ref), (1 - core, other_ref)):
            ref[:, span] = proj_ref[:, pl.ds(pl.multiple_of((2 * chip + side) * width, width), width)]


def relay_kernel(one_ref, two_ref, upper_ref, lower_ref):
    rows = upper_ref.shape[0]
    upper_ref[...] = two_ref[:rows]
    lower_ref[...] = one_ref[rows:]


def pair_kernel(own_ref, other_ref, own_proj, other_proj, kept_ref, *sent_refs):
    chip = lax.div(lax.axis_index("head"), 2)
    width = kept_ref.shape[1]
    both = cat([own_ref[...], other_ref[...]], 1)
    for step, ref in enumerate((kept_ref, *sent_refs)):
        span = pl.ds(pl.multiple_of((chip ^ step) * width, width), width)
        ref[...] = mm(both, cat([own_proj[:, span], other_proj[:, span]], 0)).astype(ref.dtype)


def own_part_kernel(own_ref, own_proj, *out_refs):
    chip = lax.div(lax.axis_index("head"), 2)
    width = own_ref.shape[1]
    for step, ref in enumerate(out_refs):
        span = pl.ds(pl.multiple_of((chip ^ step) * width, width), width)
        ref[...] = mm(own_ref[...], own_proj[:, span])


def other_part_kernel(chips, other_ref, other_proj, *refs):
    chip = lax.div(lax.axis_index("head"), 2)
    width = other_ref.shape[1]
    for step in range(chips):
        span = pl.ds(pl.multiple_of((chip ^ step) * width, width), width)
        ref = refs[chips + step]
        ref[...] = (refs[step][...] + mm(other_ref[...], other_proj[:, span])).astype(ref.dtype)


def total_of(refs):
    total = refs[0][...]
    for ref in refs[1:]:
        total = total + ref[...].astype(f32)
    return total.astype(bf16)


def add_kernel(count, *refs):
    for at in range(count):
        ref = refs[2 * count + at]
        ref[...] = (refs[at][...] + refs[count + at][...].astype(f32)).astype(ref.dtype)


def finish_kernel(*refs):
    refs[-1][...] = total_of(refs[:-1])


def finish_last_kernel(count, *refs):
    out_ref = refs[-1]
    out_ref[out_ref.shape[0] - 1] = total_of(refs[:count])
    for at, earlier in enumerate(refs[count:-1]):
        out_ref[at] = earlier[...]


VMEM = pl.BlockSpec(memory_space=pltpu.VMEM)
ANYWHERE = pl.BlockSpec(memory_space=pl.ANY)


def call(kernel, out_shape, operands, name, after=(), flops=0, scratch=()):
    count = len(operands)

    def reading(*refs):
        kernel(*refs[:count], *refs[count + len(after) :])

    return pl.pallas_call(
        reading,
        out_shape=out_shape,
        in_specs=[VMEM] * count + [ANYWHERE] * len(after),
        out_specs=jax.tree.map(lambda _: VMEM, out_shape),
        scratch_shapes=scratch,
        compiler_params=pltpu.CompilerParams(vmem_limit_bytes=VMEM_LIMIT),
        cost_estimate=pl.CostEstimate(flops=flops, bytes_accessed=0, transcendentals=0),
        name=name,
    )(*operands, *after)


def shape(dims, dtype):
    return jax.ShapeDtypeStruct(dims, dtype)


def first_message(keys, values, rates):
    _, rows, width = keys.shape
    dims = (2 * rows + RATE_ROWS, width)
    return pl.pallas_call(
        functools.partial(message_kernel, 0),
        out_shape=shape(dims, bf16),
        in_specs=[ANYWHERE, ANYWHERE, VMEM],
        out_specs=VMEM,
        scratch_shapes=[pltpu.SemaphoreType.DMA((PIECES,))],
        compiler_params=pltpu.CompilerParams(vmem_limit_bytes=MESSAGE_VMEM),
        cost_estimate=pl.CostEstimate(flops=0, bytes_accessed=0, transcendentals=0),
        name="message",
    )(keys, values, rates)


def later_message(keys, values, rates, group, after):
    _, rows, width = keys.shape
    return call(
        functools.partial(later_message_kernel, group), shape((2 * rows + RATE_ROWS, width), bf16),
        [keys, values, rates], "message", after,
    )


def shifted(value, axis, step):
    count = lax.axis_size(axis)
    return lax.ppermute(value, axis, [(at, at ^ step) for at in range(count)])


def pair(combined, own_proj, other_proj, types, after=()):
    rows, width = combined.shape
    return call(
        pair_kernel, [shape((rows, width), kind) for kind in types],
        [combined, shifted(combined, "head", 1), own_proj, other_proj], "pair", after,
    )


def to_chip(block, step):
    return shifted(block, "head", 2 * step)


def direct_sums(combined, own_proj, other_proj):
    chips = lax.axis_size("head") // 2
    rows, width = combined.shape
    other = shifted(combined, "head", 1)
    parts = call(
        own_part_kernel, [shape((rows, width), f32)] * chips, [combined, own_proj], "own_part",
        flops=UPDATE_FLOPS,
    )
    kept, *sent = call(
        functools.partial(other_part_kernel, chips),
        [shape((rows, width), f32)] + [shape((rows, width), bf16)] * (chips - 1),
        [other, other_proj, *parts], "other_part",
    )
    return [kept] + [to_chip(block, step) for step, block in enumerate(sent, 1)]


class HalvingSums:
    def __init__(self, combined, own_proj, other_proj, after):
        self.chips = lax.axis_size("head") // 2
        types = [bf16 if at % 2 else f32 for at in range(self.chips)]
        self.held = dict(enumerate(pair(combined, own_proj, other_proj, types, after)))
        self.terms = [self.held.pop(0)]
        self.marker = self.terms[0]
        self.pass_on(1)

    def pass_on(self, step):
        self.step = step
        sent = sorted((at for at in self.held if at & step), reverse=True)
        came = {at ^ step: to_chip(self.held.pop(at), step) for at in sent}
        self.terms.append(came.pop(0))
        self.came = came

    def next_step(self, after):
        step = 2 * self.step
        order = sorted(self.held)
        sums = call(
            functools.partial(add_kernel, len(order)),
            [shape(self.held[at].shape, bf16 if at & step else f32) for at in order],
            [self.held[at] for at in order] + [self.came[at] for at in order], "add", after,
        )
        self.held = dict(zip(order, sums))
        self.marker = sums[0]
        self.pass_on(step)


def opposite(one, two, after):
    rows, width = one.shape
    half = rows // 2 // 16 * 16
    upper, lower = call(
        relay_kernel, [shape((half, width), bf16), shape((rows - half, width), bf16)], [one, two], "relay", after
    )
    return shifted(upper, "ctx", 1), shifted(lower, "ctx", 2)


def body(queries, keys, values, rates, w_gate, w_up, w_down, gains, out_proj):
    groups, rows, width = queries.shape
    hidden = w_gate.shape[2]
    chips = lax.axis_size("head") // 2
    acc_shape = shape((3, width, hidden), f32)
    weight_shapes = [shape((2 * width, 2 * hidden), bf16), shape((2 * width, hidden), bf16)]
    picked = shape((width, out_proj.shape[1] // 2), bf16)

    message = first_message(keys, values, rates)
    one, two = shifted(message, "ctx", 1), shifted(message, "ctx", 2)
    acc, *weights = call(
        first_grads_kernel, [acc_shape, *weight_shapes], [message, w_gate[0], w_up[0], w_down[0]], "grads"
    )
    own_proj, for_other = call(pick_kernel, [picked, picked], [out_proj], "pick", [acc])
    other_proj = shifted(for_other, "head", 1)
    local = call(
        local_band_kernel, shape((groups, rows - WINDOW, width), f32), [queries, keys, values],
        "local_band", [own_proj],
    )
    last = past = opposite(one, two, [local])

    totals = []
    combined = None
    for g in range(groups):
        if g > 0:
            acc = call(
                functools.partial(grads_kernel, 1, False), acc_shape, [message, *weights], "grads", [combined]
            )
            last = opposite(one, two, [acc])
            totals.append(HalvingSums(combined, own_proj, other_proj, [acc]))
        acc = call(
            functools.partial(grads_kernel, 2, True), acc_shape, [one, two, *weights, acc], "grads",
            [local] if g == 0 else [totals[-1].marker],
        )
        near, after = one, []
        if g < groups - 1:
            message = later_message(keys, values, rates, g + 1, [acc])
            one, two = shifted(message, "ctx", 1), shifted(message, "ctx", 2)
            after = [message]
        acc = call(
            functools.partial(last_grads_kernel, len(last)), acc_shape, [*last, *weights, acc], "grads", after,
            scratch=[pltpu.VMEM(message.shape, bf16)],
        )
        after = [acc]
        while g > 0 and totals[-1].held:
            totals[-1].next_step(after)
            after = [totals[-1].marker]
        combined, *weights = call(
            functools.partial(update_kernel, g, (1, len(last), len(past))),
            [shape((rows, width), bf16), *weight_shapes],
            [near, *last, *past, *weights, acc, queries, keys, values, local, gains],
            "update", after, flops=UPDATE_FLOPS if g < groups - 1 else 0,
        )
        past = last
    total = direct_sums(combined, own_proj, other_proj)
    finished = [
        call(finish_kernel, shape((rows, width), bf16), earlier.terms, "finish", total[:1]) for earlier in totals
    ]
    return call(
        functools.partial(finish_last_kernel, len(total)), shape((groups, rows, width), bf16),
        [*total, *finished], "finish_last",
    )


def solution(mesh):
    return jax.shard_map(
        body,
        mesh=mesh,
        in_specs=(
            P(None, "ctx", "head"),
            P(None, "ctx", "head"),
            P(None, "ctx", "head"),
            P("head", None, "ctx"),
            P("head", None, None),
            P("head", None, None),
            P("head", None, None),
            P("head", None),
            P("head", None),
        ),
        out_specs=P(None, "ctx", "head"),
        check_vma=False,
    )
```

profile of v0, /device:TPU:8, one launch (start us, length us, event | category | flops | bytes accessed | tf_op | source)
XLA Modules:
  0.0 92.0 jit_solution(8378218902721048050)
XLA Ops:
  0.0 2.7 %message.2.refs_0_ = bf16[1040,256]{1,0:T(8,128)(2,1)} custom-call(bf16[2,512,256]{2,1,0:T(8,128)(2,1)} %refs_9_.3, bf16[2,512,256]{2,1,0:T(8,128)(2,1)} %refs_10_.3, f32[1,2,512]{2,1,0:T(2,128)} %refs_2_.3), custom_call_target="tpu_custom_call" | custom-call | tf_op jit(solution)/shard_map/message/pallas_call | solution.py:403
  2.7 1.6 %collective-permute-start.1 = (bf16[1040,256]{1,0:T(8,128)(2,1)}, bf16[1040,256]{1,0:T(8,128)(2,1)S(1)}, u32[]{:S(2)}, u32[]{:S(2)}) collective-permute-start(bf16[1040,256]{1,0:T(8,128)(2,1)} %message.2.refs_0_), channel_id=1, source_target_pairs={{0,16},{8,24},{16,0},{24,8},{1,17},{9,25},{17,1},{25,9},{2,18},{10... | collective-permute-start | bytes 1597448 | tf_op jit(solution)/shard_map/ppermute | solution.py:425
  4.3 1.5 %collective-permute-start = (bf16[1040,256]{1,0:T(8,128)(2,1)}, bf16[1040,256]{1,0:T(8,128)(2,1)S(1)}, u32[]{:S(2)}, u32[]{:S(2)}) collective-permute-start(bf16[1040,256]{1,0:T(8,128)(2,1)} %message.2.refs_0_), channel_id=1, source_target_pairs={{0,8},{8,0},{16,24},{24,16},{1,9},{9,1},{17,25},{25,17},{2,10},{10... | collective-permute-start | bytes 1597448 | tf_op jit(solution)/shard_map/ppermute | solution.py:425
  5.8 1.1 %copy-done.2 = bf16[1040,256]{1,0:T(8,128)(2,1)S(1)} copy-done((bf16[1040,256]{1,0:T(8,128)(2,1)S(1)}, bf16[1040,256]{1,0:T(8,128)(2,1)}, u32[]{:S(2)}) %copy-start.2) | copy-done | bytes 532504
  6.9 1.0 %copy-done.6 = f32[1,256,512]{2,1,0:T(8,128)S(1)} copy-done((f32[1,256,512]{2,1,0:T(8,128)S(1)}, f32[1,256,512]{2,1,0:T(8,128)}, u32[]{:S(2)}) %copy-start.6) | copy-done | bytes 524312
  9.0 2.5 %grads.6 = (f32[3,256,512]{2,1,0:T(8,128)S(1)}, bf16[512,1024]{1,0:T(8,128)(2,1)S(1)}, bf16[512,512]{1,0:T(8,128)(2,1)S(1)}) custom-call(bf16[1040,256]{1,0:T(8,128)(2,1)S(1)} %copy-done.2, f32[256,512]{1,0:T(8,128)S(1)} %bitcast.3, f32[256,512]{1,0:T(8,128)S(1)} %bitcast.4, f32[512,256]{1,0:T(8,128)S(1)} %bitcast.5), custom_call_target="tpu_custom_call" | custom-call | tf_op jit(solution)/shard_map/grads/pallas_call | solution.py:384
  13.7 3.1 %collective-permute-done.1.refs_1_ = bf16[1040,256]{1,0:T(8,128)(2,1)S(1)} collective-permute-done((bf16[1040,256]{1,0:T(8,128)(2,1)}, bf16[1040,256]{1,0:T(8,128)(2,1)S(1)}, u32[]{:S(2)}, u32[]{:S(2)}) %collective-permute-start.1) | collective-permute-done | bytes 532512 | tf_op jit(solution)/shard_map/ppermute | solution.py:425
  16.9 1.2 %collective-permute-done.refs_0_ = bf16[1040,256]{1,0:T(8,128)(2,1)S(1)} collective-permute-done((bf16[1040,256]{1,0:T(8,128)(2,1)}, bf16[1040,256]{1,0:T(8,128)(2,1)S(1)}, u32[]{:S(2)}, u32[]{:S(2)}) %collective-permute-start) | collective-permute-done | bytes 532512 | tf_op jit(solution)/shard_map/ppermute | solution.py:425
  18.7 1.5 %collective-permute-start.4 = (bf16[512,256]{1,0:T(8,128)(2,1)S(1)}, bf16[512,256]{1,0:T(8,128)(2,1)S(1)}, u32[]{:S(2)}, u32[]{:S(2)}) collective-permute-start(bf16[512,256]{1,0:T(8,128)(2,1)S(1)} %get-tuple-element.34), channel_id=1, source_target_pairs={{0,8},{8,0},{16,24},{24,16},{1,9},{9,1},{17,25},{25,17},{2,10},{10... | collective-permute-start | bytes 786440 | tf_op jit(solution)/shard_map/ppermute | solution.py:425
  20.2 4.5 %grads.7.refs_3_.refs_4_ = f32[3,256,512]{2,1,0:T(8,128)S(1)} custom-call(bf16[1040,256]{1,0:T(8,128)(2,1)S(1)} %collective-permute-done.refs_0_, bf16[1040,256]{1,0:T(8,128)(2,1)S(1)} %collective-permute-done.1.refs_1_, bf16[512,1024]{1,0:T(8,128)(2,1)S(1)} %get-tuple-element.30.refs_2_.refs_5_, bf16[512,512]{1,0:T(8,128)(2,1)S(1)} %get-tuple-element.31.refs_3_.refs_6_, ...), custom_call_target="tpu_custom_call" | custom-call | tf_op jit(solution)/shard_map/grads/pallas_call | solution.py:384
  24.9 1.6 %collective-permute-start.3 = (bf16[1040,256]{1,0:T(8,128)(2,1)S(1)}, bf16[1040,256]{1,0:T(8,128)(2,1)S(1)}, u32[]{:S(2)}, u32[]{:S(2)}) collective-permute-start(bf16[1040,256]{1,0:T(8,128)(2,1)S(1)} %message.3.refs_5_.refs_0_), channel_id=1, source_target_pairs={{0,16},{8,24},{16,0},{24,8},{1,17},{9,25},{17,1},{25,9},{2,18},{10... | collective-permute-start | bytes 1597448 | tf_op jit(solution)/shard_map/ppermute | solution.py:425
  27.0 2.3 %grads.8.refs_7_.refs_13_ = f32[3,256,512]{2,1,0:T(8,128)S(1)} custom-call(bf16[512,256]{1,0:T(8,128)(2,1)S(1)} %collective-permute-done.4.refs_0_.refs_1_.refs_3_, bf16[528,256]{1,0:T(8,128)(2,1)S(1)} %collective-permute-done.5.refs_1_.refs_2_.refs_4_, bf16[512,1024]{1,0:T(8,128)(2,1)S(1)} %get-tuple-element.30.refs_2_.refs_5_, ...), custom_call_target="tpu_custom_call" | custom-call | tf_op jit(solution)/shard_map/grads/pallas_call | solution.py:384
  29.3 8.0 %update.2 = (bf16[512,256]{1,0:T(8,128)(2,1)S(1)}, bf16[512,1024]{1,0:T(8,128)(2,1)S(1)}, bf16[512,512]{1,0:T(8,128)(2,1)S(1)}) custom-call(bf16[1040,256]{1,0:T(8,128)(2,1)S(1)} %collective-permute-done.refs_0_, bf16[512,256]{1,0:T(8,128)(2,1)S(1)} %collective-permute-done.4.refs_0_.refs_1_.refs_3_, ...), custom_call_target="tpu_custom_call" | custom-call | flops 30000001024 | tf_op jit(solution)/shard_map/update/pallas_call | solution.py:384
  37.4 2.5 %grads.9.refs_2_.refs_4_ = f32[3,256,512]{2,1,0:T(8,128)S(1)} custom-call(bf16[1040,256]{1,0:T(8,128)(2,1)S(1)} %message.3.refs_5_.refs_0_, bf16[512,1024]{1,0:T(8,128)(2,1)S(1)} %get-tuple-element.36.refs_1_.refs_2_.refs_5_, bf16[512,512]{1,0:T(8,128)(2,1)S(1)} %get-tuple-element.37.refs_2_.refs_3_.refs_6_, ...), custom_call_target="tpu_custom_call" | custom-call | tf_op jit(solution)/shard_map/grads/pallas_call | solution.py:384
  43.2 1.6 %collective-permute-start.15 = (bf16[512,256]{1,0:T(8,128)(2,1)S(1)}, bf16[512,256]{1,0:T(8,128)(2,1)S(1)}, u32[]{:S(2)}, u32[]{:S(2)}) collective-permute-start(bf16[512,256]{1,0:T(8,128)(2,1)S(1)} %get-tuple-element.54), channel_id=1, source_target_pairs={{0,2},{1,3},{2,0},{3,1},{4,6},{5,7},{6,4},{7,5},{8,10},{9,11},{10,... | collective-permute-start | bytes 786440 | tf_op jit(solution)/shard_map/ppermute | solution.py:425
  44.8 4.7 %grads.10.refs_4_ = f32[3,256,512]{2,1,0:T(8,128)S(1)} custom-call(bf16[1040,256]{1,0:T(8,128)(2,1)S(1)} %collective-permute-done.2.refs_0_, bf16[1040,256]{1,0:T(8,128)(2,1)S(1)} %collective-permute-done.3.refs_1_, bf16[512,1024]{1,0:T(8,128)(2,1)S(1)} %get-tuple-element.36.refs_1_.refs_2_.refs_5_, ...), custom_call_target="tpu_custom_call" | custom-call | tf_op jit(solution)/shard_map/grads/pallas_call | solution.py:384
  49.5 2.3 %grads.11.refs_2_.refs_7_ = f32[3,256,512]{2,1,0:T(8,128)S(1)} custom-call(bf16[512,256]{1,0:T(8,128)(2,1)S(1)} %collective-permute-done.6.refs_0_.refs_1_, bf16[528,256]{1,0:T(8,128)(2,1)S(1)} %collective-permute-done.7.refs_1_.refs_2_, bf16[512,1024]{1,0:T(8,128)(2,1)S(1)} %get-tuple-element.36.refs_1_.refs_2_.refs_5_, ...), custom_call_target="tpu_custom_call" | custom-call | tf_op jit(solution)/shard_map/grads/pallas_call | solution.py:384
  52.0 2.7 %collective-permute-start.16 = (bf16[512,256]{1,0:T(8,128)(2,1)S(1)}, bf16[512,256]{1,0:T(8,128)(2,1)S(1)}, u32[]{:S(2)}, u32[]{:S(2)}) collective-permute-start(bf16[512,256]{1,0:T(8,128)(2,1)S(1)} %add.1.refs_13_), channel_id=1, source_target_pairs={{0,4},{1,5},{2,6},{3,7},{4,0},{5,1},{6,2},{7,3},{8,12},{9,13},{10,... | collective-permute-start | bytes 786440 | tf_op jit(solution)/shard_map/ppermute | solution.py:425
  54.7 7.7 %update.3 = (bf16[512,256]{1,0:T(8,128)(2,1)S(1)}, bf16[512,1024]{1,0:T(8,128)(2,1)}, bf16[512,512]{1,0:T(8,128)(2,1)}) custom-call(bf16[1040,256]{1,0:T(8,128)(2,1)S(1)} %collective-permute-done.2.refs_0_, bf16[512,256]{1,0:T(8,128)(2,1)S(1)} %collective-permute-done.6.refs_0_.refs_1_, bf16[528,256]{1,0:T(8,128)(2,1)S(1)} %collective-permute-done.7.refs_1_.refs_2_, ...), custom_call_target="tpu_custom_call" | custom-call | tf_op jit(solution)/shard_map/update/pallas_call | solution.py:384
  63.0 1.1 %collective-permute-done.11.refs_0_ = bf16[512,256]{1,0:T(8,128)(2,1)S(1)} collective-permute-done((bf16[512,256]{1,0:T(8,128)(2,1)S(1)}, bf16[512,256]{1,0:T(8,128)(2,1)S(1)}, u32[]{:S(2)}, u32[]{:S(2)}) %collective-permute-start.11) | collective-permute-done | bytes 262176 | tf_op jit(solution)/shard_map/ppermute | solution.py:425
  65.4 2.7 %collective-permute-start.14 = (bf16[512,256]{1,0:T(8,128)(2,1)S(1)}, bf16[512,256]{1,0:T(8,128)(2,1)S(1)}, u32[]{:S(2)}, u32[]{:S(2)}) collective-permute-start(bf16[512,256]{1,0:T(8,128)(2,1)S(1)} %get-tuple-element.53), channel_id=1, source_target_pairs={{0,6},{1,7},{2,4},{3,5},{4,2},{5,3},{6,0},{7,1},{8,14},{9,15},{10,... | collective-permute-start | bytes 786440 | tf_op jit(solution)/shard_map/ppermute | solution.py:425
  68.2 6.0 %collective-permute-done.12.refs_1_ = bf16[512,256]{1,0:T(8,128)(2,1)S(1)} collective-permute-done((bf16[512,256]{1,0:T(8,128)(2,1)S(1)}, bf16[512,256]{1,0:T(8,128)(2,1)S(1)}, u32[]{:S(2)}, u32[]{:S(2)}) %collective-permute-start.12) | collective-permute-done | bytes 262176 | tf_op jit(solution)/shard_map/ppermute | solution.py:425
  74.2 4.1 %collective-permute-done.13.refs_2_ = bf16[512,256]{1,0:T(8,128)(2,1)S(1)} collective-permute-done((bf16[512,256]{1,0:T(8,128)(2,1)S(1)}, bf16[512,256]{1,0:T(8,128)(2,1)S(1)}, u32[]{:S(2)}, u32[]{:S(2)}) %collective-permute-start.13) | collective-permute-done | bytes 262176 | tf_op jit(solution)/shard_map/ppermute | solution.py:425
  78.2 12.8 %collective-permute-done.14.refs_3_ = bf16[512,256]{1,0:T(8,128)(2,1)S(1)} collective-permute-done((bf16[512,256]{1,0:T(8,128)(2,1)S(1)}, bf16[512,256]{1,0:T(8,128)(2,1)S(1)}, u32[]{:S(2)}, u32[]{:S(2)}) %collective-permute-start.14) | collective-permute-done | bytes 262176 | tf_op jit(solution)/shard_map/ppermute | solution.py:425
  (50 shorter events, 11.0 us)
Async XLA Ops:
  0.0 5.8 %copy-start.5 = (f32[1,256,512]{2,1,0:T(8,128)S(1)}, f32[1,256,512]{2,1,0:T(8,128)}, u32[]{:S(2)}) copy-start(f32[1,256,512]{2,1,0:T(8,128)} %param.13) | copy-start | bytes 1572868
  0.0 11.6 %copy-start.4 = (bf16[256,2048]{1,0:T(8,128)(2,1)S(1)}, bf16[256,2048]{1,0:T(8,128)(2,1)}, u32[]{:S(2)}) copy-start(bf16[256,2048]{1,0:T(8,128)(2,1)} %refs_0_.3) | copy-start | bytes 3145732
  2.7 14.1 %collective-permute-start.1 = (bf16[1040,256]{1,0:T(8,128)(2,1)}, bf16[1040,256]{1,0:T(8,128)(2,1)S(1)}, u32[]{:S(2)}, u32[]{:S(2)}) collective-permute-start(bf16[1040,256]{1,0:T(8,128)(2,1)} %message.2.refs_0_), channel_id=1, source_target_pairs={{0,16},{8,24},{16,0},{24,8},{1,17},{9,25},{17,1},{25,9},{2,18},{10... | collective-permute-start | bytes 1597448 | tf_op jit(solution)/shard_map/ppermute | solution.py:425
  4.3 13.8 %collective-permute-start = (bf16[1040,256]{1,0:T(8,128)(2,1)}, bf16[1040,256]{1,0:T(8,128)(2,1)S(1)}, u32[]{:S(2)}, u32[]{:S(2)}) collective-permute-start(bf16[1040,256]{1,0:T(8,128)(2,1)} %message.2.refs_0_), channel_id=1, source_target_pairs={{0,8},{8,0},{16,24},{24,16},{1,9},{9,1},{17,25},{25,17},{2,10},{10... | collective-permute-start | bytes 1597448 | tf_op jit(solution)/shard_map/ppermute | solution.py:425
  5.8 1.1 %copy-start.2 = (bf16[1040,256]{1,0:T(8,128)(2,1)S(1)}, bf16[1040,256]{1,0:T(8,128)(2,1)}, u32[]{:S(2)}) copy-start(bf16[1040,256]{1,0:T(8,128)(2,1)} %message.2.refs_0_) | copy-start | bytes 1597444
  11.6 1.2 %copy-start.1 = (bf16[2,512,256]{2,1,0:T(8,128)(2,1)S(1)}, bf16[2,512,256]{2,1,0:T(8,128)(2,1)}, u32[]{:S(2)}) copy-start(bf16[2,512,256]{2,1,0:T(8,128)(2,1)} %refs_10_.3) | copy-start | bytes 1572868
  11.6 1.3 %copy-start.3 = (bf16[2,512,256]{2,1,0:T(8,128)(2,1)S(1)}, bf16[2,512,256]{2,1,0:T(8,128)(2,1)}, u32[]{:S(2)}) copy-start(bf16[2,512,256]{2,1,0:T(8,128)(2,1)} %refs_8_.3) | copy-start | bytes 1572868
  18.1 8.8 %collective-permute-start.5 = (bf16[528,256]{1,0:T(8,128)(2,1)S(1)}, bf16[528,256]{1,0:T(8,128)(2,1)S(1)}, u32[]{:S(2)}, u32[]{:S(2)}) collective-permute-start(bf16[528,256]{1,0:T(8,128)(2,1)S(1)} %get-tuple-element.35), channel_id=1, source_target_pairs={{0,16},{8,24},{16,0},{24,8},{1,17},{9,25},{17,1},{25,9},{2,18},{10... | collective-permute-start | bytes 811016 | tf_op jit(solution)/shard_map/ppermute | solution.py:425
  18.7 8.3 %collective-permute-start.4 = (bf16[512,256]{1,0:T(8,128)(2,1)S(1)}, bf16[512,256]{1,0:T(8,128)(2,1)S(1)}, u32[]{:S(2)}, u32[]{:S(2)}) collective-permute-start(bf16[512,256]{1,0:T(8,128)(2,1)S(1)} %get-tuple-element.34), channel_id=1, source_target_pairs={{0,8},{8,0},{16,24},{24,16},{1,9},{9,1},{17,25},{25,17},{2,10},{10... | collective-permute-start | bytes 786440 | tf_op jit(solution)/shard_map/ppermute | solution.py:425
  20.2 21.8 %collective-permute-start.9 = (bf16[256,1024]{1,0:T(8,128)(2,1)S(1)}, bf16[256,1024]{1,0:T(8,128)(2,1)S(1)}, u32[]{:S(2)}, u32[]{:S(2)}) collective-permute-start(bf16[256,1024]{1,0:T(8,128)(2,1)S(1)} %get-tuple-element.41), channel_id=1, source_target_pairs={{0,1},{1,0},{2,3},{3,2},{4,5},{5,4},{6,7},{7,6},{8,9},{9,8},{10,11... | collective-permute-start | bytes 1572872 | tf_op jit(solution)/shard_map/ppermute | solution.py:425
  20.2 4.6 %copy-start.8 = (f32[1,2,512]{2,1,0:T(2,128)S(1)}, f32[1,2,512]{2,1,0:T(2,128)}, u32[]{:S(2)}) copy-start(f32[1,2,512]{2,1,0:T(2,128)} %refs_2_.3) | copy-start | bytes 12292
  24.8 4.5 %copy-start.9 = (f32[1,256]{1,0:T(1,128)S(1)}, f32[1,256]{1,0:T(1,128)}, u32[]{:S(2)}) copy-start(f32[1,256]{1,0:T(1,128)} %refs_12_.3) | copy-start | bytes 3076
  24.9 15.0 %collective-permute-start.3 = (bf16[1040,256]{1,0:T(8,128)(2,1)S(1)}, bf16[1040,256]{1,0:T(8,128)(2,1)S(1)}, u32[]{:S(2)}, u32[]{:S(2)}) collective-permute-start(bf16[1040,256]{1,0:T(8,128)(2,1)S(1)} %message.3.refs_5_.refs_0_), channel_id=1, source_target_pairs={{0,16},{8,24},{16,0},{24,8},{1,17},{9,25},{17,1},{25,9},{2,18},{10... | collective-permute-start | bytes 1597448 | tf_op jit(solution)/shard_map/ppermute | solution.py:425
  26.4 14.2 %collective-permute-start.2 = (bf16[1040,256]{1,0:T(8,128)(2,1)S(1)}, bf16[1040,256]{1,0:T(8,128)(2,1)S(1)}, u32[]{:S(2)}, u32[]{:S(2)}) collective-permute-start(bf16[1040,256]{1,0:T(8,128)(2,1)S(1)} %message.3.refs_5_.refs_0_), channel_id=1, source_target_pairs={{0,8},{8,0},{16,24},{24,16},{1,9},{9,1},{17,25},{25,17},{2,10},{10... | collective-permute-start | bytes 1597448 | tf_op jit(solution)/shard_map/ppermute | solution.py:425
  37.3 4.7 %collective-permute-start.8 = (bf16[512,256]{1,0:T(8,128)(2,1)S(1)}, bf16[512,256]{1,0:T(8,128)(2,1)S(1)}, u32[]{:S(2)}, u32[]{:S(2)}) collective-permute-start(bf16[512,256]{1,0:T(8,128)(2,1)S(1)} %get-tuple-element.38.refs_3_.refs_0_), channel_id=1, source_target_pairs={{0,1},{1,0},{2,3},{3,2},{4,5},{5,4},{6,7},{7,6},{8,9},{9,8},{10,11... | collective-permute-start | bytes 786440 | tf_op jit(solution)/shard_map/ppermute | solution.py:425
  40.7 8.8 %collective-permute-start.7 = (bf16[528,256]{1,0:T(8,128)(2,1)S(1)}, bf16[528,256]{1,0:T(8,128)(2,1)S(1)}, u32[]{:S(2)}, u32[]{:S(2)}) collective-permute-start(bf16[528,256]{1,0:T(8,128)(2,1)S(1)} %get-tuple-element.40), channel_id=1, source_target_pairs={{0,16},{8,24},{16,0},{24,8},{1,17},{9,25},{17,1},{25,9},{2,18},{10... | collective-permute-start | bytes 811016 | tf_op jit(solution)/shard_map/ppermute | solution.py:425
  41.3 8.2 %collective-permute-start.6 = (bf16[512,256]{1,0:T(8,128)(2,1)S(1)}, bf16[512,256]{1,0:T(8,128)(2,1)S(1)}, u32[]{:S(2)}, u32[]{:S(2)}) collective-permute-start(bf16[512,256]{1,0:T(8,128)(2,1)S(1)} %get-tuple-element.39), channel_id=1, source_target_pairs={{0,8},{8,0},{16,24},{24,16},{1,9},{9,1},{17,25},{25,17},{2,10},{10... | collective-permute-start | bytes 786440 | tf_op jit(solution)/shard_map/ppermute | solution.py:425
  42.7 9.3 %collective-permute-start.10 = (bf16[512,256]{1,0:T(8,128)(2,1)S(1)}, bf16[512,256]{1,0:T(8,128)(2,1)S(1)}, u32[]{:S(2)}, u32[]{:S(2)}) collective-permute-start(bf16[512,256]{1,0:T(8,128)(2,1)S(1)} %get-tuple-element.44), channel_id=1, source_target_pairs={{0,2},{1,3},{2,0},{3,1},{4,6},{5,7},{6,4},{7,5},{8,10},{9,11},{10,... | collective-permute-start | bytes 786440 | tf_op jit(solution)/shard_map/ppermute | solution.py:425
  43.2 24.8 %collective-permute-start.15 = (bf16[512,256]{1,0:T(8,128)(2,1)S(1)}, bf16[512,256]{1,0:T(8,128)(2,1)S(1)}, u32[]{:S(2)}, u32[]{:S(2)}) collective-permute-start(bf16[512,256]{1,0:T(8,128)(2,1)S(1)} %get-tuple-element.54), channel_id=1, source_target_pairs={{0,2},{1,3},{2,0},{3,1},{4,6},{5,7},{6,4},{7,5},{8,10},{9,11},{10,... | collective-permute-start | bytes 786440 | tf_op jit(solution)/shard_map/ppermute | solution.py:425
  52.0 16.1 %collective-permute-start.16 = (bf16[512,256]{1,0:T(8,128)(2,1)S(1)}, bf16[512,256]{1,0:T(8,128)(2,1)S(1)}, u32[]{:S(2)}, u32[]{:S(2)}) collective-permute-start(bf16[512,256]{1,0:T(8,128)(2,1)S(1)} %add.1.refs_13_), channel_id=1, source_target_pairs={{0,4},{1,5},{2,6},{3,7},{4,0},{5,1},{6,2},{7,3},{8,12},{9,13},{10,... | collective-permute-start | bytes 786440 | tf_op jit(solution)/shard_map/ppermute | solution.py:425
  62.5 1.6 %collective-permute-start.11 = (bf16[512,256]{1,0:T(8,128)(2,1)S(1)}, bf16[512,256]{1,0:T(8,128)(2,1)S(1)}, u32[]{:S(2)}, u32[]{:S(2)}) collective-permute-start(bf16[512,256]{1,0:T(8,128)(2,1)S(1)} %get-tuple-element.45.refs_0_), channel_id=1, source_target_pairs={{0,1},{1,0},{2,3},{3,2},{4,5},{5,4},{6,7},{7,6},{8,9},{9,8},{10,11... | collective-permute-start | bytes 786440 | tf_op jit(solution)/shard_map/ppermute | solution.py:425
  64.5 9.6 %collective-permute-start.12 = (bf16[512,256]{1,0:T(8,128)(2,1)S(1)}, bf16[512,256]{1,0:T(8,128)(2,1)S(1)}, u32[]{:S(2)}, u32[]{:S(2)}) collective-permute-start(bf16[512,256]{1,0:T(8,128)(2,1)S(1)} %get-tuple-element.51), channel_id=1, source_target_pairs={{0,2},{1,3},{2,0},{3,1},{4,6},{5,7},{6,4},{7,5},{8,10},{9,11},{10,... | collective-permute-start | bytes 786440 | tf_op jit(solution)/shard_map/ppermute | solution.py:425
  65.1 13.2 %collective-permute-start.13 = (bf16[512,256]{1,0:T(8,128)(2,1)S(1)}, bf16[512,256]{1,0:T(8,128)(2,1)S(1)}, u32[]{:S(2)}, u32[]{:S(2)}) collective-permute-start(bf16[512,256]{1,0:T(8,128)(2,1)S(1)} %get-tuple-element.52), channel_id=1, source_target_pairs={{0,4},{1,5},{2,6},{3,7},{4,0},{5,1},{6,2},{7,3},{8,12},{9,13},{10,... | collective-permute-start | bytes 786440 | tf_op jit(solution)/shard_map/ppermute | solution.py:425
  65.4 25.6 %collective-permute-start.14 = (bf16[512,256]{1,0:T(8,128)(2,1)S(1)}, bf16[512,256]{1,0:T(8,128)(2,1)S(1)}, u32[]{:S(2)}, u32[]{:S(2)}) collective-permute-start(bf16[512,256]{1,0:T(8,128)(2,1)S(1)} %get-tuple-element.53), channel_id=1, source_target_pairs={{0,6},{1,7},{2,4},{3,5},{4,2},{5,3},{6,0},{7,1},{8,14},{9,15},{10,... | collective-permute-start | bytes 786440 | tf_op jit(solution)/shard_map/ppermute | solution.py:425
  (3 other events, 3.1 us)
where the time goes:
time: 92.3 us; the launch traced here: 92 us
  Pallas kernels  41.1 us (45%)
  waiting for transfers between devices  29.2 us (32%)
  starting transfers between devices  17 us (18%)
  local copies, waits for them, and re-layouts  4.34 us (5%)
    pallas_call x19, Pallas kernels, call(): pl.pallas_call(reading, out_shape=out_shape, in_specs=[VMEM] * count + [A...  38.4 us
    ppermute x17, waiting for transfers between devices, shifted(): return lax.ppermute(value, axis, [(at, at ^ step) for at in range(count)])  29.2 us
    ppermute x17, starting transfers between devices, shifted(): return lax.ppermute(value, axis, [(at, at ^ step) for at in range(count)])  17 us
    unnamed x20, local copies, waits for them, and re-layouts  4.34 us
    pallas_call x1, Pallas kernels, first_message(): pl.pallas_call(functools.partial(message_kernel, 0), out_shape=shape(dims...  2.74 us
  transfers between devices with their start and end apart: 17, of which 8 were waited for; matrix products, arithmetic and copies ran while one was open for 0% of the time, Pallas kernels for 41%

commit v1 on v0

--- a/solution.py
+++ b/solution.py
@@ -11,7 +11,6 @@
 NS_ITERS = 5
 RATE_ROWS = 16
 VMEM_LIMIT = 20 * 1024 * 1024
-PIECES = 8
 UPDATE_FLOPS = 30_000_000_000
 MESSAGE_VMEM = 60 * 1024 * 1024
 
@@ -75,42 +74,67 @@
 TOKEN_TILE = 256
 
 
-def add_chunk(acc, key_ref, value_ref, rate_ref, gate_up_ref, down_turned_ref):
+def add_messages(acc, messages, gate_up_ref, down_turned_ref):
     hidden_width = down_turned_ref.shape[1]
-    tiles = value_ref.shape[0] // TOKEN_TILE
-    rate = rate_column(rate_ref[...], tiles)
-    state = [{} for _ in range(tiles)]
+    block = min(256, hidden_width)
+    blocks = [slice(at, at + block) for at in range(0, hidden_width, block)]
+    sums = [[None if part is None else part[:, span] for span in blocks] for part in acc]
+    tiles = []
+    for message in messages:
+        key_ref, value_ref, rate_ref = message_parts(message)
+        count = value_ref.shape[0] // TOKEN_TILE
+        rate = rate_column(rate_ref[...], count)
+        for at in range(count):
+            tiles.append((key_ref, value_ref, rate, slice(at * TOKEN_TILE, at * TOKEN_TILE + TOKEN_TILE)))
+    state = [{} for _ in tiles]
 
     def forward(at):
+        key_ref, value_ref, rate, rows = tiles[at]
         tile = state[at]
-        rows = slice(at * TOKEN_TILE, at * TOKEN_TILE + TOKEN_TILE)
         keys, values = key_ref[rows], value_ref[rows]
         tile["rate"], tile["scale"] = rate[rows], unit_scale(keys)
-        tile["keys"], tile["values"] = keys.T, values.T
-        tile["pre"] = mm(cat([keys, keys], 1), gate_up_ref[...])
-        tile["back"] = mm(cat([values, values], 1), down_turned_ref[...])
+        both_keys, both_values = cat([keys, keys], 1), cat([values, values], 1)
+        tile["pre"] = []
+        for span in blocks:
+            gate_pre = mm(both_keys, gate_up_ref[:, span])
+            yield
+            up_pre = mm(both_keys, gate_up_ref[:, hidden_width + span.start : hidden_width + span.stop])
+            yield
+            tile["pre"].append((gate_pre, up_pre, mm(both_values, down_turned_ref[:, span])))
+            yield
+        tile["turned"] = [part.T for part in (keys, keys, values)]
+        yield
 
     def middle(at):
         tile = state[at]
-        pre = tile["pre"] * tile["scale"]
-        gate_pre, up_pre = pre[:, :hidden_width], pre[:, hidden_width:]
-        sigma, gate_act = silu_parts(gate_pre)
-        back = tile["back"] * (tile["rate"] * tile["scale"])
-        slope = sigma + gate_act * (1.0 - sigma)
-        terms = (back * up_pre * slope, back * gate_act, gate_act * up_pre * tile["rate"])
-        tile["terms"] = [cat(split(term), 0) for term in terms]
+        tile["terms"] = []
+        for gate_pre, up_pre, back in tile["pre"]:
+            gate_pre, up_pre = gate_pre * tile["scale"], up_pre * tile["scale"]
+            sigma, gate_act = silu_parts(gate_pre)
+            back = back * (tile["rate"] * tile["scale"])
+            slope = sigma + gate_act * (1.0 - sigma)
+            terms = (back * up_pre * slope, back * gate_act, gate_act * up_pre * tile["rate"])
+            tile["terms"].append([term.astype(bf16) for term in terms])
+            yield
 
     def backward(at):
         tile = state[at]
-        turned = [cat([tile[name]] * 2, 1) for name in ("keys", "keys", "values")]
-        for place, (left, right) in enumerate(zip(turned, tile["terms"])):
-            part = mm(left, right)
-            acc[place] = part if acc[place] is None else acc[place] + part
-
-    for step in range(tiles + 2):
-        for lag, stage in enumerate((forward, middle, backward)):
-            if 0 <= step - lag < tiles:
-                stage(step - lag)
+        for column, terms in enumerate(tile["terms"]):
+            for place, (left, right) in enumerate(zip(tile["turned"], terms)):
+                part, before = mm(left, right), sums[place][column]
+                sums[place][column] = part if before is None else before + part
+                yield
+
+    for step in range(len(tiles) + 2):
+        stages = [
+            stage(step - lag)
+            for lag, stage in ((2, backward), (1, middle), (0, forward))
+            if 0 <= step - lag < len(tiles)
+        ]
+        while stages:
+            stages = [stage for stage in stages if next(stage, True) is None]
+    for place in range(3):
+        acc[place] = cat(sums[place], 1)
 
 
 NS_PASSES = (1, 1, 3, 3, 3)
@@ -193,20 +217,11 @@
     return tile.astype(bf16)
 
 
-def message_kernel(group, keys_ref, values_ref, rates_ref, out_ref, sems):
-    rows = keys_ref.shape[1]
-    piece = 2 * rows // PIECES
-    copies = []
-    for at in range(PIECES):
-        start = at * piece
-        source = keys_ref if start < rows else values_ref
-        copies.append(pltpu.make_async_copy(
-            source.at[group, pl.ds(start % rows, piece)], out_ref.at[pl.ds(start, piece)], sems.at[at]
-        ))
-        copies[-1].start()
+def message_kernel(group, keys_ref, values_ref, rates_ref, out_ref):
+    rows = keys_ref.shape[0]
+    out_ref[:rows] = keys_ref[...]
+    out_ref[rows : 2 * rows] = values_ref[...]
     out_ref[2 * rows :] = rate_tile(rates_ref, group, rows // 256)
-    for copy in copies:
-        copy.wait()
 
 
 def later_message_kernel(group, keys_ref, values_ref, rates_ref, out_ref):
@@ -238,7 +253,7 @@
     gate_up_ref[...] = stacked_split(cat([gate_ref[...], up_ref[...]], 1))
     down_turned_ref[...] = stacked_split(down_ref[...].T)
     acc = [None] * 3
-    add_chunk(acc, *message_parts(message), gate_up_ref, down_turned_ref)
+    add_messages(acc, [message], gate_up_ref, down_turned_ref)
     for at in range(3):
         out_ref[at] = acc[at]
 
@@ -248,8 +263,7 @@
     gate_up_ref, down_turned_ref = refs[:2]
     out_ref = refs[-1]
     acc = [refs[2][at] for at in range(3)] if carried else [None] * 3
-    for message in messages:
-        add_chunk(acc, *message_parts(message), gate_up_ref, down_turned_ref)
+    add_messages(acc, messages, gate_up_ref, down_turned_ref)
     for at in range(3):
         out_ref[at] = acc[at]
 
@@ -261,7 +275,7 @@
         held[start : start + ref.shape[0]] = ref[...]
         start += ref.shape[0]
     acc = [acc_ref[at] for at in range(3)]
-    add_chunk(acc, *message_parts(held), gate_up_ref, down_turned_ref)
+    add_messages(acc, [held], gate_up_ref, down_turned_ref)
     for at in range(3):
         out_ref[at] = acc[at]
 
@@ -400,12 +414,13 @@
 def first_message(keys, values, rates):
     _, rows, width = keys.shape
     dims = (2 * rows + RATE_ROWS, width)
+    block = pl.BlockSpec((None, rows, width), lambda step: (0, 0, 0))
     return pl.pallas_call(
         functools.partial(message_kernel, 0),
         out_shape=shape(dims, bf16),
-        in_specs=[ANYWHERE, ANYWHERE, VMEM],
-        out_specs=VMEM,
-        scratch_shapes=[pltpu.SemaphoreType.DMA((PIECES,))],
+        grid=(1,),
+        in_specs=[block, block, pl.BlockSpec(rates.shape, lambda step: (0, 0, 0))],
+        out_specs=pl.BlockSpec(dims, lambda step: (0, 0)),
         compiler_params=pltpu.CompilerParams(vmem_limit_bytes=MESSAGE_VMEM),
         cost_estimate=pl.CostEstimate(flops=0, bytes_accessed=0, transcendentals=0),
         name="message",
@@ -450,7 +465,8 @@
         [shape((rows, width), f32)] + [shape((rows, width), bf16)] * (chips - 1),
         [other, other_proj, *parts], "other_part",
     )
-    return [kept] + [to_chip(block, step) for step, block in enumerate(sent, 1)]
+    order = [*range(2, chips), 1]
+    return [kept] + [to_chip(sent[step - 1], step) for step in order]
 
 
 class HalvingSums:
@@ -519,8 +535,8 @@
             acc = call(
                 functools.partial(grads_kernel, 1, False), acc_shape, [message, *weights], "grads", [combined]
             )
-            last = opposite(one, two, [acc])
             totals.append(HalvingSums(combined, own_proj, other_proj, [acc]))
+            last = opposite(one, two, [totals[-1].marker])
         acc = call(
             functools.partial(grads_kernel, 2, True), acc_shape, [one, two, *weights, acc], "grads",
             [local] if g == 0 else [totals[-1].marker],

time: 92.3 us -> 88.5 us (0.959)
  Pallas kernels: 41.1 us -> 36 us
    pallas_call x19, Pallas kernels: 38.4 us -> 34 us  [call(): pl.pallas_call(reading, out_shape=out_shape, in_specs=[VMEM] * count + [A...]
  transfers between devices with their start and end apart: 17 -> 17, of which waited for: 8 -> 8; matrix products, arithmetic and copies ran while one was open for 0% -> 0% of each run, Pallas kernels for 41% -> 37%
where the time goes in v1:
time: 88.5 us; the launch traced here: 88.2 us
  Pallas kernels  36 us (41%)
  waiting for transfers between devices  29.9 us (34%)
  starting transfers between devices  17.8 us (20%)
  local copies, waits for them, and re-layouts  4.34 us (5%)
    pallas_call x19, Pallas kernels, call(): pl.pallas_call(reading, out_shape=out_shape, in_specs=[VMEM] * count + [A...  34 us
    ppermute x17, waiting for transfers between devices, shifted(): return lax.ppermute(value, axis, [(at, at ^ step) for at in range(count)])  29.9 us
    ppermute x17, starting transfers between devices, shifted(): return lax.ppermute(value, axis, [(at, at ^ step) for at in range(count)])  17.8 us
    unnamed x20, local copies, waits for them, and re-layouts  4.34 us
    pallas_call x1, Pallas kernels, first_message(): pl.pallas_call(functools.partial(message_kernel, 0), out_shape=shape(dims...  2 us
  transfers between devices with their start and end apart: 17, of which 8 were waited for; matrix products, arithmetic and copies ran while one was open for 0% of the time, Pallas kernels for 37%

profile of v1, /device:TPU:8, one launch (start us, length us, event | category | flops | bytes accessed | tf_op | source)
XLA Modules:
  0.0 88.2 jit_solution(10660373690772865014)
XLA Ops:
  0.0 2.0 %message.2.refs_0_ = bf16[1040,256]{1,0:T(8,128)(2,1)} custom-call(bf16[2,512,256]{2,1,0:T(8,128)(2,1)} %refs_9_.3, bf16[2,512,256]{2,1,0:T(8,128)(2,1)} %refs_10_.3, f32[1,2,512]{2,1,0:T(2,128)} %refs_2_.3), custom_call_target="tpu_custom_call" | custom-call | tf_op jit(solution)/shard_map/message/pallas_call | solution.py:418
  2.0 1.5 %collective-permute-start.1 = (bf16[1040,256]{1,0:T(8,128)(2,1)}, bf16[1040,256]{1,0:T(8,128)(2,1)S(1)}, u32[]{:S(2)}, u32[]{:S(2)}) collective-permute-start(bf16[1040,256]{1,0:T(8,128)(2,1)} %message.2.refs_0_), channel_id=1, source_target_pairs={{0,16},{8,24},{16,0},{24,8},{1,17},{9,25},{17,1},{25,9},{2,18},{10... | collective-permute-start | bytes 1597448 | tf_op jit(solution)/shard_map/ppermute | solution.py:440
  3.5 1.5 %collective-permute-start = (bf16[1040,256]{1,0:T(8,128)(2,1)}, bf16[1040,256]{1,0:T(8,128)(2,1)S(1)}, u32[]{:S(2)}, u32[]{:S(2)}) collective-permute-start(bf16[1040,256]{1,0:T(8,128)(2,1)} %message.2.refs_0_), channel_id=1, source_target_pairs={{0,8},{8,0},{16,24},{24,16},{1,9},{9,1},{17,25},{25,17},{2,10},{10... | collective-permute-start | bytes 1597448 | tf_op jit(solution)/shard_map/ppermute | solution.py:440
  5.0 1.1 %copy-done.2 = bf16[1040,256]{1,0:T(8,128)(2,1)S(1)} copy-done((bf16[1040,256]{1,0:T(8,128)(2,1)S(1)}, bf16[1040,256]{1,0:T(8,128)(2,1)}, u32[]{:S(2)}) %copy-start.2) | copy-done | bytes 532504
  8.2 1.9 %grads.6 = (f32[3,256,512]{2,1,0:T(8,128)S(1)}, bf16[512,1024]{1,0:T(8,128)(2,1)S(1)}, bf16[512,512]{1,0:T(8,128)(2,1)S(1)}) custom-call(bf16[1040,256]{1,0:T(8,128)(2,1)S(1)} %copy-done.2, f32[256,512]{1,0:T(8,128)S(1)} %bitcast.3, f32[256,512]{1,0:T(8,128)S(1)} %bitcast.4, f32[512,256]{1,0:T(8,128)S(1)} %bitcast.5), custom_call_target="tpu_custom_call" | custom-call | tf_op jit(solution)/shard_map/grads/pallas_call | solution.py:398
  12.3 3.8 %collective-permute-done.1.refs_1_ = bf16[1040,256]{1,0:T(8,128)(2,1)S(1)} collective-permute-done((bf16[1040,256]{1,0:T(8,128)(2,1)}, bf16[1040,256]{1,0:T(8,128)(2,1)S(1)}, u32[]{:S(2)}, u32[]{:S(2)}) %collective-permute-start.1) | collective-permute-done | bytes 532512 | tf_op jit(solution)/shard_map/ppermute | solution.py:440
  16.1 1.2 %collective-permute-done.refs_0_ = bf16[1040,256]{1,0:T(8,128)(2,1)S(1)} collective-permute-done((bf16[1040,256]{1,0:T(8,128)(2,1)}, bf16[1040,256]{1,0:T(8,128)(2,1)S(1)}, u32[]{:S(2)}, u32[]{:S(2)}) %collective-permute-start) | collective-permute-done | bytes 532512 | tf_op jit(solution)/shard_map/ppermute | solution.py:440
  17.9 1.5 %collective-permute-start.4 = (bf16[512,256]{1,0:T(8,128)(2,1)S(1)}, bf16[512,256]{1,0:T(8,128)(2,1)S(1)}, u32[]{:S(2)}, u32[]{:S(2)}) collective-permute-start(bf16[512,256]{1,0:T(8,128)(2,1)S(1)} %get-tuple-element.34), channel_id=1, source_target_pairs={{0,8},{8,0},{16,24},{24,16},{1,9},{9,1},{17,25},{25,17},{2,10},{10... | collective-permute-start | bytes 786440 | tf_op jit(solution)/shard_map/ppermute | solution.py:440
  19.4 3.5 %grads.7.refs_3_.refs_4_ = f32[3,256,512]{2,1,0:T(8,128)S(1)} custom-call(bf16[1040,256]{1,0:T(8,128)(2,1)S(1)} %collective-permute-done.refs_0_, bf16[1040,256]{1,0:T(8,128)(2,1)S(1)} %collective-permute-done.1.refs_1_, bf16[512,1024]{1,0:T(8,128)(2,1)S(1)} %get-tuple-element.30.refs_2_.refs_5_, bf16[512,512]{1,0:T(8,128)(2,1)S(1)} %get-tuple-element.31.refs_3_.refs_6_, ...), custom_call_target="tpu_custom_call" | custom-call | tf_op jit(solution)/shard_map/grads/pallas_call | solution.py:398
  23.0 1.6 %collective-permute-start.3 = (bf16[1040,256]{1,0:T(8,128)(2,1)S(1)}, bf16[1040,256]{1,0:T(8,128)(2,1)S(1)}, u32[]{:S(2)}, u32[]{:S(2)}) collective-permute-start(bf16[1040,256]{1,0:T(8,128)(2,1)S(1)} %message.3.refs_5_.refs_0_), channel_id=1, source_target_pairs={{0,16},{8,24},{16,0},{24,8},{1,17},{9,25},{17,1},{25,9},{2,18},{10... | collective-permute-start | bytes 1597448 | tf_op jit(solution)/shard_map/ppermute | solution.py:440
  25.1 1.8 %grads.8.refs_7_.refs_13_ = f32[3,256,512]{2,1,0:T(8,128)S(1)} custom-call(bf16[512,256]{1,0:T(8,128)(2,1)S(1)} %collective-permute-done.4.refs_0_.refs_1_.refs_3_, bf16[528,256]{1,0:T(8,128)(2,1)S(1)} %collective-permute-done.5.refs_1_.refs_2_.refs_4_, bf16[512,1024]{1,0:T(8,128)(2,1)S(1)} %get-tuple-element.30.refs_2_.refs_5_, ...), custom_call_target="tpu_custom_call" | custom-call | tf_op jit(solution)/shard_map/grads/pallas_call | solution.py:398
  27.0 8.0 %update.2 = (bf16[512,256]{1,0:T(8,128)(2,1)S(1)}, bf16[512,1024]{1,0:T(8,128)(2,1)S(1)}, bf16[512,512]{1,0:T(8,128)(2,1)S(1)}) custom-call(bf16[1040,256]{1,0:T(8,128)(2,1)S(1)} %collective-permute-done.refs_0_, bf16[512,256]{1,0:T(8,128)(2,1)S(1)} %collective-permute-done.4.refs_0_.refs_1_.refs_3_, ...), custom_call_target="tpu_custom_call" | custom-call | flops 30000001024 | tf_op jit(solution)/shard_map/update/pallas_call | solution.py:398
  35.0 1.8 %grads.9.refs_4_ = f32[3,256,512]{2,1,0:T(8,128)S(1)} custom-call(bf16[1040,256]{1,0:T(8,128)(2,1)S(1)} %message.3.refs_5_.refs_0_, bf16[512,1024]{1,0:T(8,128)(2,1)S(1)} %get-tuple-element.38.refs_1_.refs_2_.refs_5_, bf16[512,512]{1,0:T(8,128)(2,1)S(1)} %get-tuple-element.39.refs_2_.refs_3_.refs_6_, bf16[512,256]{1,0:T(8,128)(2,1)S(1)} %get-tuple-element.36.refs_3_.refs_0_), custom_call_target="tpu_custom_call" | custom-call | tf_op jit(solution)/shard_map/grads/pallas_call | solution.py:398
  37.6 1.2 %collective-permute-done.2.refs_0_ = bf16[1040,256]{1,0:T(8,128)(2,1)S(1)} collective-permute-done((bf16[1040,256]{1,0:T(8,128)(2,1)S(1)}, bf16[1040,256]{1,0:T(8,128)(2,1)S(1)}, u32[]{:S(2)}, u32[]{:S(2)}) %collective-permute-start.2) | collective-permute-done | bytes 532512 | tf_op jit(solution)/shard_map/ppermute | solution.py:440
  40.6 1.6 %collective-permute-start.15 = (bf16[512,256]{1,0:T(8,128)(2,1)S(1)}, bf16[512,256]{1,0:T(8,128)(2,1)S(1)}, u32[]{:S(2)}, u32[]{:S(2)}) collective-permute-start(bf16[512,256]{1,0:T(8,128)(2,1)S(1)} %get-tuple-element.54), channel_id=1, source_target_pairs={{0,2},{1,3},{2,0},{3,1},{4,6},{5,7},{6,4},{7,5},{8,10},{9,11},{10,... | collective-permute-start | bytes 786440 | tf_op jit(solution)/shard_map/ppermute | solution.py:440
  42.2 3.4 %grads.10.refs_4_ = f32[3,256,512]{2,1,0:T(8,128)S(1)} custom-call(bf16[1040,256]{1,0:T(8,128)(2,1)S(1)} %collective-permute-done.2.refs_0_, bf16[1040,256]{1,0:T(8,128)(2,1)S(1)} %collective-permute-done.3.refs_1_, bf16[512,1024]{1,0:T(8,128)(2,1)S(1)} %get-tuple-element.38.refs_1_.refs_2_.refs_5_, ...), custom_call_target="tpu_custom_call" | custom-call | tf_op jit(solution)/shard_map/grads/pallas_call | solution.py:398
  45.5 1.5 %collective-permute-done.8.refs_0_.refs_1_ = bf16[512,256]{1,0:T(8,128)(2,1)S(1)} collective-permute-done((bf16[512,256]{1,0:T(8,128)(2,1)S(1)}, bf16[512,256]{1,0:T(8,128)(2,1)S(1)}, u32[]{:S(2)}, u32[]{:S(2)}) %collective-permute-start.8) | collective-permute-done | bytes 262176 | tf_op jit(solution)/shard_map/ppermute | solution.py:440
  47.1 1.8 %grads.11.refs_2_.refs_7_ = f32[3,256,512]{2,1,0:T(8,128)S(1)} custom-call(bf16[512,256]{1,0:T(8,128)(2,1)S(1)} %collective-permute-done.8.refs_0_.refs_1_, bf16[528,256]{1,0:T(8,128)(2,1)S(1)} %collective-permute-done.9.refs_1_.refs_2_, bf16[512,1024]{1,0:T(8,128)(2,1)S(1)} %get-tuple-element.38.refs_1_.refs_2_.refs_5_, ...), custom_call_target="tpu_custom_call" | custom-call | tf_op jit(solution)/shard_map/grads/pallas_call | solution.py:398
  49.4 2.7 %collective-permute-start.16 = (bf16[512,256]{1,0:T(8,128)(2,1)S(1)}, bf16[512,256]{1,0:T(8,128)(2,1)S(1)}, u32[]{:S(2)}, u32[]{:S(2)}) collective-permute-start(bf16[512,256]{1,0:T(8,128)(2,1)S(1)} %add.1.refs_13_), channel_id=1, source_target_pairs={{0,4},{1,5},{2,6},{3,7},{4,0},{5,1},{6,2},{7,3},{8,12},{9,13},{10,... | collective-permute-start | bytes 786440 | tf_op jit(solution)/shard_map/ppermute | solution.py:440
  52.0 8.0 %update.3 = (bf16[512,256]{1,0:T(8,128)(2,1)S(1)}, bf16[512,1024]{1,0:T(8,128)(2,1)}, bf16[512,512]{1,0:T(8,128)(2,1)}) custom-call(bf16[1040,256]{1,0:T(8,128)(2,1)S(1)} %collective-permute-done.2.refs_0_, bf16[512,256]{1,0:T(8,128)(2,1)S(1)} %collective-permute-done.8.refs_0_.refs_1_, bf16[528,256]{1,0:T(8,128)(2,1)S(1)} %collective-permute-done.9.refs_1_.refs_2_, ...), custom_call_target="tpu_custom_call" | custom-call | tf_op jit(solution)/shard_map/update/pallas_call | solution.py:398
  62.5 1.6 %collective-permute-start.13 = (bf16[512,256]{1,0:T(8,128)(2,1)S(1)}, bf16[512,256]{1,0:T(8,128)(2,1)S(1)}, u32[]{:S(2)}, u32[]{:S(2)}) collective-permute-start(bf16[512,256]{1,0:T(8,128)(2,1)S(1)} %get-tuple-element.52), channel_id=1, source_target_pairs={{0,6},{1,7},{2,4},{3,5},{4,2},{5,3},{6,0},{7,1},{8,14},{9,15},{10,... | collective-permute-start | bytes 786440 | tf_op jit(solution)/shard_map/ppermute | solution.py:440
  64.1 2.5 %collective-permute-start.14 = (bf16[512,256]{1,0:T(8,128)(2,1)S(1)}, bf16[512,256]{1,0:T(8,128)(2,1)S(1)}, u32[]{:S(2)}, u32[]{:S(2)}) collective-permute-start(bf16[512,256]{1,0:T(8,128)(2,1)S(1)} %get-tuple-element.53), channel_id=1, source_target_pairs={{0,2},{1,3},{2,0},{3,1},{4,6},{5,7},{6,4},{7,5},{8,10},{9,11},{10,... | collective-permute-start | bytes 786440 | tf_op jit(solution)/shard_map/ppermute | solution.py:440
  66.7 12.9 %collective-permute-done.12.refs_1_ = bf16[512,256]{1,0:T(8,128)(2,1)S(1)} collective-permute-done((bf16[512,256]{1,0:T(8,128)(2,1)S(1)}, bf16[512,256]{1,0:T(8,128)(2,1)S(1)}, u32[]{:S(2)}, u32[]{:S(2)}) %collective-permute-start.12) | collective-permute-done | bytes 262176 | tf_op jit(solution)/shard_map/ppermute | solution.py:440
  79.6 7.7 %collective-permute-done.13.refs_2_ = bf16[512,256]{1,0:T(8,128)(2,1)S(1)} collective-permute-done((bf16[512,256]{1,0:T(8,128)(2,1)S(1)}, bf16[512,256]{1,0:T(8,128)(2,1)S(1)}, u32[]{:S(2)}, u32[]{:S(2)}) %collective-permute-start.13) | collective-permute-done | bytes 262176 | tf_op jit(solution)/shard_map/ppermute | solution.py:440
  (50 shorter events, 12.0 us)
Async XLA Ops:
  0.0 5.0 %copy-start.5 = (f32[1,256,512]{2,1,0:T(8,128)S(1)}, f32[1,256,512]{2,1,0:T(8,128)}, u32[]{:S(2)}) copy-start(f32[1,256,512]{2,1,0:T(8,128)} %param.13) | copy-start | bytes 1572868
  0.0 10.1 %copy-start.4 = (bf16[256,2048]{1,0:T(8,128)(2,1)S(1)}, bf16[256,2048]{1,0:T(8,128)(2,1)}, u32[]{:S(2)}) copy-start(bf16[256,2048]{1,0:T(8,128)(2,1)} %refs_0_.3) | copy-start | bytes 3145732
  2.0 14.0 %collective-permute-start.1 = (bf16[1040,256]{1,0:T(8,128)(2,1)}, bf16[1040,256]{1,0:T(8,128)(2,1)S(1)}, u32[]{:S(2)}, u32[]{:S(2)}) collective-permute-start(bf16[1040,256]{1,0:T(8,128)(2,1)} %message.2.refs_0_), channel_id=1, source_target_pairs={{0,16},{8,24},{16,0},{24,8},{1,17},{9,25},{17,1},{25,9},{2,18},{10... | collective-permute-start | bytes 1597448 | tf_op jit(solution)/shard_map/ppermute | solution.py:440
  3.5 13.8 %collective-permute-start = (bf16[1040,256]{1,0:T(8,128)(2,1)}, bf16[1040,256]{1,0:T(8,128)(2,1)S(1)}, u32[]{:S(2)}, u32[]{:S(2)}) collective-permute-start(bf16[1040,256]{1,0:T(8,128)(2,1)} %message.2.refs_0_), channel_id=1, source_target_pairs={{0,8},{8,0},{16,24},{24,16},{1,9},{9,1},{17,25},{25,17},{2,10},{10... | collective-permute-start | bytes 1597448 | tf_op jit(solution)/shard_map/ppermute | solution.py:440
  5.0 1.1 %copy-start.2 = (bf16[1040,256]{1,0:T(8,128)(2,1)S(1)}, bf16[1040,256]{1,0:T(8,128)(2,1)}, u32[]{:S(2)}) copy-start(bf16[1040,256]{1,0:T(8,128)(2,1)} %message.2.refs_0_) | copy-start | bytes 1597444
  10.1 1.2 %copy-start.1 = (bf16[2,512,256]{2,1,0:T(8,128)(2,1)S(1)}, bf16[2,512,256]{2,1,0:T(8,128)(2,1)}, u32[]{:S(2)}) copy-start(bf16[2,512,256]{2,1,0:T(8,128)(2,1)} %refs_10_.3) | copy-start | bytes 1572868
  10.1 1.3 %copy-start.3 = (bf16[2,512,256]{2,1,0:T(8,128)(2,1)S(1)}, bf16[2,512,256]{2,1,0:T(8,128)(2,1)}, u32[]{:S(2)}) copy-start(bf16[2,512,256]{2,1,0:T(8,128)(2,1)} %refs_8_.3) | copy-start | bytes 1572868
  17.3 7.8 %collective-permute-start.5 = (bf16[528,256]{1,0:T(8,128)(2,1)S(1)}, bf16[528,256]{1,0:T(8,128)(2,1)S(1)}, u32[]{:S(2)}, u32[]{:S(2)}) collective-permute-start(bf16[528,256]{1,0:T(8,128)(2,1)S(1)} %get-tuple-element.35), channel_id=1, source_target_pairs={{0,16},{8,24},{16,0},{24,8},{1,17},{9,25},{17,1},{25,9},{2,18},{10... | collective-permute-start | bytes 811016 | tf_op jit(solution)/shard_map/ppermute | solution.py:440
  17.9 7.2 %collective-permute-start.4 = (bf16[512,256]{1,0:T(8,128)(2,1)S(1)}, bf16[512,256]{1,0:T(8,128)(2,1)S(1)}, u32[]{:S(2)}, u32[]{:S(2)}) collective-permute-start(bf16[512,256]{1,0:T(8,128)(2,1)S(1)} %get-tuple-element.34), channel_id=1, source_target_pairs={{0,8},{8,0},{16,24},{24,16},{1,9},{9,1},{17,25},{25,17},{2,10},{10... | collective-permute-start | bytes 786440 | tf_op jit(solution)/shard_map/ppermute | solution.py:440
  19.4 17.5 %collective-permute-start.7 = (bf16[256,1024]{1,0:T(8,128)(2,1)S(1)}, bf16[256,1024]{1,0:T(8,128)(2,1)S(1)}, u32[]{:S(2)}, u32[]{:S(2)}) collective-permute-start(bf16[256,1024]{1,0:T(8,128)(2,1)S(1)} %get-tuple-element.37), channel_id=1, source_target_pairs={{0,1},{1,0},{2,3},{3,2},{4,5},{5,4},{6,7},{7,6},{8,9},{9,8},{10,11... | collective-permute-start | bytes 1572872 | tf_op jit(solution)/shard_map/ppermute | solution.py:440
  19.4 3.5 %copy-start.8 = (f32[1,2,512]{2,1,0:T(2,128)S(1)}, f32[1,2,512]{2,1,0:T(2,128)}, u32[]{:S(2)}) copy-start(f32[1,2,512]{2,1,0:T(2,128)} %refs_2_.3) | copy-start | bytes 12292
  23.0 4.0 %copy-start.9 = (f32[1,256]{1,0:T(1,128)S(1)}, f32[1,256]{1,0:T(1,128)}, u32[]{:S(2)}) copy-start(f32[1,256]{1,0:T(1,128)} %refs_12_.3) | copy-start | bytes 3076
  23.0 14.6 %collective-permute-start.3 = (bf16[1040,256]{1,0:T(8,128)(2,1)S(1)}, bf16[1040,256]{1,0:T(8,128)(2,1)S(1)}, u32[]{:S(2)}, u32[]{:S(2)}) collective-permute-start(bf16[1040,256]{1,0:T(8,128)(2,1)S(1)} %message.3.refs_5_.refs_0_), channel_id=1, source_target_pairs={{0,16},{8,24},{16,0},{24,8},{1,17},{9,25},{17,1},{25,9},{2,18},{10... | collective-permute-start | bytes 1597448 | tf_op jit(solution)/shard_map/ppermute | solution.py:440
  24.6 14.2 %collective-permute-start.2 = (bf16[1040,256]{1,0:T(8,128)(2,1)S(1)}, bf16[1040,256]{1,0:T(8,128)(2,1)S(1)}, u32[]{:S(2)}, u32[]{:S(2)}) collective-permute-start(bf16[1040,256]{1,0:T(8,128)(2,1)S(1)} %message.3.refs_5_.refs_0_), channel_id=1, source_target_pairs={{0,8},{8,0},{16,24},{24,16},{1,9},{9,1},{17,25},{25,17},{2,10},{10... | collective-permute-start | bytes 1597448 | tf_op jit(solution)/shard_map/ppermute | solution.py:440
  35.0 1.9 %collective-permute-start.6 = (bf16[512,256]{1,0:T(8,128)(2,1)S(1)}, bf16[512,256]{1,0:T(8,128)(2,1)S(1)}, u32[]{:S(2)}, u32[]{:S(2)}) collective-permute-start(bf16[512,256]{1,0:T(8,128)(2,1)S(1)} %get-tuple-element.36.refs_3_.refs_0_), channel_id=1, source_target_pairs={{0,1},{1,0},{2,3},{3,2},{4,5},{5,4},{6,7},{7,6},{8,9},{9,8},{10,11... | collective-permute-start | bytes 786440 | tf_op jit(solution)/shard_map/ppermute | solution.py:440
  38.9 8.2 %collective-permute-start.9 = (bf16[528,256]{1,0:T(8,128)(2,1)S(1)}, bf16[528,256]{1,0:T(8,128)(2,1)S(1)}, u32[]{:S(2)}, u32[]{:S(2)}) collective-permute-start(bf16[528,256]{1,0:T(8,128)(2,1)S(1)} %get-tuple-element.42), channel_id=1, source_target_pairs={{0,16},{8,24},{16,0},{24,8},{1,17},{9,25},{17,1},{25,9},{2,18},{10... | collective-permute-start | bytes 811016 | tf_op jit(solution)/shard_map/ppermute | solution.py:440
  39.4 7.7 %collective-permute-start.8 = (bf16[512,256]{1,0:T(8,128)(2,1)S(1)}, bf16[512,256]{1,0:T(8,128)(2,1)S(1)}, u32[]{:S(2)}, u32[]{:S(2)}) collective-permute-start(bf16[512,256]{1,0:T(8,128)(2,1)S(1)} %get-tuple-element.41), channel_id=1, source_target_pairs={{0,8},{8,0},{16,24},{24,16},{1,9},{9,1},{17,25},{25,17},{2,10},{10... | collective-permute-start | bytes 786440 | tf_op jit(solution)/shard_map/ppermute | solution.py:440
  40.1 9.2 %collective-permute-start.10 = (bf16[512,256]{1,0:T(8,128)(2,1)S(1)}, bf16[512,256]{1,0:T(8,128)(2,1)S(1)}, u32[]{:S(2)}, u32[]{:S(2)}) collective-permute-start(bf16[512,256]{1,0:T(8,128)(2,1)S(1)} %get-tuple-element.44), channel_id=1, source_target_pairs={{0,2},{1,3},{2,0},{3,1},{4,6},{5,7},{6,4},{7,5},{8,10},{9,11},{10,... | collective-permute-start | bytes 786440 | tf_op jit(solution)/shard_map/ppermute | solution.py:440
  40.6 26.0 %collective-permute-start.15 = (bf16[512,256]{1,0:T(8,128)(2,1)S(1)}, bf16[512,256]{1,0:T(8,128)(2,1)S(1)}, u32[]{:S(2)}, u32[]{:S(2)}) collective-permute-start(bf16[512,256]{1,0:T(8,128)(2,1)S(1)} %get-tuple-element.54), channel_id=1, source_target_pairs={{0,2},{1,3},{2,0},{3,1},{4,6},{5,7},{6,4},{7,5},{8,10},{9,11},{10,... | collective-permute-start | bytes 786440 | tf_op jit(solution)/shard_map/ppermute | solution.py:440
  49.4 17.2 %collective-permute-start.16 = (bf16[512,256]{1,0:T(8,128)(2,1)S(1)}, bf16[512,256]{1,0:T(8,128)(2,1)S(1)}, u32[]{:S(2)}, u32[]{:S(2)}) collective-permute-start(bf16[512,256]{1,0:T(8,128)(2,1)S(1)} %add.1.refs_13_), channel_id=1, source_target_pairs={{0,4},{1,5},{2,6},{3,7},{4,0},{5,1},{6,2},{7,3},{8,12},{9,13},{10,... | collective-permute-start | bytes 786440 | tf_op jit(solution)/shard_map/ppermute | solution.py:440
  60.0 1.6 %collective-permute-start.11 = (bf16[512,256]{1,0:T(8,128)(2,1)S(1)}, bf16[512,256]{1,0:T(8,128)(2,1)S(1)}, u32[]{:S(2)}, u32[]{:S(2)}) collective-permute-start(bf16[512,256]{1,0:T(8,128)(2,1)S(1)} %get-tuple-element.45.refs_0_), channel_id=1, source_target_pairs={{0,1},{1,0},{2,3},{3,2},{4,5},{5,4},{6,7},{7,6},{8,9},{9,8},{10,11... | collective-permute-start | bytes 786440 | tf_op jit(solution)/shard_map/ppermute | solution.py:440
  62.1 17.5 %collective-permute-start.12 = (bf16[512,256]{1,0:T(8,128)(2,1)S(1)}, bf16[512,256]{1,0:T(8,128)(2,1)S(1)}, u32[]{:S(2)}, u32[]{:S(2)}) collective-permute-start(bf16[512,256]{1,0:T(8,128)(2,1)S(1)} %get-tuple-element.51), channel_id=1, source_target_pairs={{0,4},{1,5},{2,6},{3,7},{4,0},{5,1},{6,2},{7,3},{8,12},{9,13},{10,... | collective-permute-start | bytes 786440 | tf_op jit(solution)/shard_map/ppermute | solution.py:440
  62.5 24.8 %collective-permute-start.13 = (bf16[512,256]{1,0:T(8,128)(2,1)S(1)}, bf16[512,256]{1,0:T(8,128)(2,1)S(1)}, u32[]{:S(2)}, u32[]{:S(2)}) collective-permute-start(bf16[512,256]{1,0:T(8,128)(2,1)S(1)} %get-tuple-element.52), channel_id=1, source_target_pairs={{0,6},{1,7},{2,4},{3,5},{4,2},{5,3},{6,0},{7,1},{8,14},{9,15},{10,... | collective-permute-start | bytes 786440 | tf_op jit(solution)/shard_map/ppermute | solution.py:440
  64.1 23.2 %collective-permute-start.14 = (bf16[512,256]{1,0:T(8,128)(2,1)S(1)}, bf16[512,256]{1,0:T(8,128)(2,1)S(1)}, u32[]{:S(2)}, u32[]{:S(2)}) collective-permute-start(bf16[512,256]{1,0:T(8,128)(2,1)S(1)} %get-tuple-element.53), channel_id=1, source_target_pairs={{0,2},{1,3},{2,0},{3,1},{4,6},{5,7},{6,4},{7,5},{8,10},{9,11},{10,... | collective-permute-start | bytes 786440 | tf_op jit(solution)/shard_map/ppermute | solution.py:440
  (3 other events, 3.1 us)

commit v2 on v1

--- a/solution.py
+++ b/solution.py
@@ -12,6 +12,7 @@
 RATE_ROWS = 16
 VMEM_LIMIT = 20 * 1024 * 1024
 UPDATE_FLOPS = 30_000_000_000
+LAST_PIECES = 4
 MESSAGE_VMEM = 60 * 1024 * 1024
 
 attn_temp = 5.0
@@ -162,13 +163,16 @@
     return mm(left[0], right[0]) if len(left) == 1 else mm_split(left, right)
 
 
-def orthogonal(grads):
+def orthogonal(grads, beside):
     iterates = [
         grad * (1.0 / (jnp.sqrt(jnp.sum(grad * grad, keepdims=True)) + 1e-06)) for grad in grads
     ]
     for passes in NS_PASSES:
         parts = [parts_of(iterate, passes) for iterate in iterates]
         grams = [gram_of(part) for part in parts]
+        if passes > 1 and beside is not None:
+            beside()
+            beside = None
         squares = [square_of(parts_of(gram, passes)) for gram in grams]
         polys = [quintic_two * gram + quintic_three * square for gram, square in zip(grams, squares)]
         iterates = [
@@ -271,7 +275,7 @@
 def last_grads_kernel(parts, *refs):
     gate_up_ref, down_turned_ref, acc_ref, out_ref, held = refs[parts:]
     start = 0
-    for ref in refs[:parts]:
+    for ref in reversed(refs[:parts]):
         held[start : start + ref.shape[0]] = ref[...]
         start += ref.shape[0]
     acc = [acc_ref[at] for at in range(3)]
@@ -283,7 +287,7 @@
 def tails(refs, rows):
     found = []
     for end in (rows, 2 * rows):
-        for ref in refs:
+        for ref in reversed(refs):
             if end <= ref.shape[0]:
                 found.append(ref[end - WINDOW : end])
                 break
@@ -297,9 +301,6 @@
     past, refs = refs[: counts[2]], refs[counts[2] :]
     gate_up_ref, down_turned_ref, acc_ref, queries_ref, keys_ref, values_ref, local_ref, gains_ref, *refs = refs
     out_ref, gate_up_out, down_turned_out = refs
-    ortho = orthogonal([acc_ref[at] for at in range(3)])
-    gate_up_out[...] = stacked_split(joined(gate_up_ref) + step_size * cat(ortho[:2], 1))
-    down_turned_out[...] = stacked_split(joined(down_turned_ref) + step_size * ortho[2])
     rows = queries_ref.shape[1]
     query_rows = queries_ref.at[group]
     place = lax.axis_index("ctx")
@@ -308,14 +309,21 @@
     halo = [jnp.where(is_near, *pair) for pair in zip(tails(near, rows), tails(last, rows))]
     if group > 0:
         halo = [jnp.where(is_first, *pair) for pair in zip(tails(past, rows), halo)]
-    head_block = band(
-        query_rows[:WINDOW],
-        cat([halo[0], keys_ref[group, :WINDOW]], 0),
-        cat([halo[1], values_ref[group, :WINDOW]], 0),
-        is_first if group == 0 else None,
-    )
+    head_block = []
+
+    def attend():
+        head_block.append(band(
+            query_rows[:WINDOW],
+            cat([halo[0], keys_ref[group, :WINDOW]], 0),
+            cat([halo[1], values_ref[group, :WINDOW]], 0),
+            is_first if group == 0 else None,
+        ))
+
+    ortho = orthogonal([acc_ref[at] for at in range(3)], attend)
+    gate_up_out[...] = stacked_split(joined(gate_up_ref) + step_size * cat(ortho[:2], 1))
+    down_turned_out[...] = stacked_split(joined(down_turned_ref) + step_size * ortho[2])
     normed = apply_fast(query_rows[...], gate_up_out[...], down_turned_out[...], gains_ref[...])
-    out_ref[:WINDOW] = (head_block + normed[:WINDOW]).astype(bf16)
+    out_ref[:WINDOW] = (head_block[0] + normed[:WINDOW]).astype(bf16)
     if rows > WINDOW:
         out_ref[WINDOW:] = (local_ref[group] + normed[WINDOW:]).astype(bf16)
 
@@ -329,10 +337,8 @@
             ref[:, span] = proj_ref[:, pl.ds(pl.multiple_of((2 * chip + side) * width, width), width)]
 
 
-def relay_kernel(one_ref, two_ref, upper_ref, lower_ref):
-    rows = upper_ref.shape[0]
-    upper_ref[...] = two_ref[:rows]
-    lower_ref[...] = one_ref[rows:]
+def relay_kernel(start, message_ref, part_ref):
+    part_ref[...] = message_ref[start : start + part_ref.shape[0]]
 
 
 def pair_kernel(own_ref, other_ref, own_proj, other_proj, kept_ref, *sent_refs):
@@ -379,17 +385,29 @@
 
 
 def finish_last_kernel(count, *refs):
-    out_ref = refs[-1]
-    out_ref[out_ref.shape[0] - 1] = total_of(refs[:count])
-    for at, earlier in enumerate(refs[count:-1]):
-        out_ref[at] = earlier[...]
+    out_ref, held, sems = refs[-3:]
+    terms, earlier = refs[:count], refs[count:-3]
+    last = out_ref.shape[0] - 1
+    copies = [
+        pltpu.make_async_copy(ref, out_ref.at[at], sems.at[at]) for at, ref in enumerate(earlier)
+    ]
+    piece = held.shape[0] // LAST_PIECES
+    for copy in copies:
+        copy.start()
+    for at in range(LAST_PIECES):
+        rows = pl.ds(at * piece, piece)
+        held[rows] = total_of([term.at[rows] for term in terms])
+        copies.append(pltpu.make_async_copy(held.at[rows], out_ref.at[last, rows], sems.at[last + at]))
+        copies[-1].start()
+    for copy in copies:
+        copy.wait()
 
 
 VMEM = pl.BlockSpec(memory_space=pltpu.VMEM)
 ANYWHERE = pl.BlockSpec(memory_space=pl.ANY)
 
 
-def call(kernel, out_shape, operands, name, after=(), flops=0, scratch=()):
+def call(kernel, out_shape, operands, name, after=(), flops=0, scratch=(), out=VMEM):
     count = len(operands)
 
     def reading(*refs):
@@ -399,7 +417,7 @@
         reading,
         out_shape=out_shape,
         in_specs=[VMEM] * count + [ANYWHERE] * len(after),
-        out_specs=jax.tree.map(lambda _: VMEM, out_shape),
+        out_specs=jax.tree.map(lambda _: out, out_shape),
         scratch_shapes=scratch,
         compiler_params=pltpu.CompilerParams(vmem_limit_bytes=VMEM_LIMIT),
         cost_estimate=pl.CostEstimate(flops=flops, bytes_accessed=0, transcendentals=0),
@@ -500,11 +518,13 @@
 
 def opposite(one, two, after):
     rows, width = one.shape
-    half = rows // 2 // 16 * 16
-    upper, lower = call(
-        relay_kernel, [shape((half, width), bf16), shape((rows - half, width), bf16)], [one, two], "relay", after
-    )
-    return shifted(upper, "ctx", 1), shifted(lower, "ctx", 2)
+    half = (rows // 2 + 15) // 16 * 16
+    upper = call(functools.partial(relay_kernel, 0), shape((half, width), bf16), [two], "relay", after)
+    lower = call(
+        functools.partial(relay_kernel, half), shape((rows - half, width), bf16), [one], "relay", [upper]
+    )
+    lower = shifted(lower, "ctx", 2)
+    return lower, shifted(upper, "ctx", 1)
 
 
 def body(queries, keys, values, rates, w_gate, w_up, w_down, gains, out_proj):
@@ -554,11 +574,13 @@
         while g > 0 and totals[-1].held:
             totals[-1].next_step(after)
             after = [totals[-1].marker]
+        outs, scratch = [shape((rows, width), bf16), *weight_shapes], []
+        if g == groups - 1:
+            outs, scratch = outs[:1], [pltpu.VMEM(kept.shape, kept.dtype) for kept in weight_shapes]
         combined, *weights = call(
-            functools.partial(update_kernel, g, (1, len(last), len(past))),
-            [shape((rows, width), bf16), *weight_shapes],
+            functools.partial(update_kernel, g, (1, len(last), len(past))), outs,
             [near, *last, *past, *weights, acc, queries, keys, values, local, gains],
-            "update", after, flops=UPDATE_FLOPS if g < groups - 1 else 0,
+            "update", after, flops=UPDATE_FLOPS if g < groups - 1 else 0, scratch=scratch,
         )
         past = last
     total = direct_sums(combined, own_proj, other_proj)
@@ -567,7 +589,8 @@
     ]
     return call(
         functools.partial(finish_last_kernel, len(total)), shape((groups, rows, width), bf16),
-        [*total, *finished], "finish_last",
+        [*total, *finished], "finish_last", out=ANYWHERE,
+        scratch=[pltpu.VMEM((rows, width), bf16), pltpu.SemaphoreType.DMA((groups - 1 + LAST_PIECES,))],
     )
 
 

time: 88.5 us -> 87.8 us (level)
  waiting for transfers between devices: 29.9 us -> 28 us
  starting transfers between devices: 17.8 us -> 19.2 us
    ppermute x17, waiting for transfers between devices: 29.9 us -> 28 us  [shifted(): return lax.ppermute(value, axis, [(at, at ^ step) for at in range(count)])]
    ppermute x17, starting transfers between devices: 17.8 us -> 19.2 us  [shifted(): return lax.ppermute(value, axis, [(at, at ^ step) for at in range(count)])]
    pallas_call x19 -> x21, Pallas kernels: 34 us -> 33.6 us  [call(): pl.pallas_call(reading, out_shape=out_shape, in_specs=[VMEM] * count + [A...]
where the time goes in v2:
time: 87.8 us; the launch traced here: 87.5 us
  Pallas kernels  35.6 us (41%)
  waiting for transfers between devices  28 us (32%)
  starting transfers between devices  19.2 us (22%)
  local copies, waits for them, and re-layouts  4.34 us (5%)
    pallas_call x21, Pallas kernels, call(): pl.pallas_call(reading, out_shape=out_shape, in_specs=[VMEM] * count + [A...  33.6 us
    ppermute x17, waiting for transfers between devices, shifted(): return lax.ppermute(value, axis, [(at, at ^ step) for at in range(count)])  28 us
    ppermute x17, starting transfers between devices, shifted(): return lax.ppermute(value, axis, [(at, at ^ step) for at in range(count)])  19.2 us
    unnamed x20, local copies, waits for them, and re-layouts  4.34 us
    pallas_call x1, Pallas kernels, first_message(): pl.pallas_call(functools.partial(message_kernel, 0), out_shape=shape(dims...  2.01 us
  transfers between devices with their start and end apart: 17, of which 8 were waited for; matrix products, arithmetic and copies ran while one was open for 0% of the time, Pallas kernels for 37%

profile of v2, /device:TPU:8, one launch (start us, length us, event | category | flops | bytes accessed | tf_op | source)
XLA Modules:
  0.0 87.5 jit_solution(12815917310338002814)
XLA Ops:
  0.0 2.0 %message.2.refs_0_ = bf16[1040,256]{1,0:T(8,128)(2,1)} custom-call(bf16[2,512,256]{2,1,0:T(8,128)(2,1)} %refs_9_.3, bf16[2,512,256]{2,1,0:T(8,128)(2,1)} %refs_10_.3, f32[1,2,512]{2,1,0:T(2,128)} %refs_2_.3), custom_call_target="tpu_custom_call" | custom-call | tf_op jit(solution)/shard_map/message/pallas_call | solution.py:436
  2.0 1.5 %collective-permute-start.1 = (bf16[1040,256]{1,0:T(8,128)(2,1)}, bf16[1040,256]{1,0:T(8,128)(2,1)S(1)}, u32[]{:S(2)}, u32[]{:S(2)}) collective-permute-start(bf16[1040,256]{1,0:T(8,128)(2,1)} %message.2.refs_0_), channel_id=1, source_target_pairs={{0,16},{8,24},{16,0},{24,8},{1,17},{9,25},{17,1},{25,9},{2,18},{10... | collective-permute-start | bytes 1597448 | tf_op jit(solution)/shard_map/ppermute | solution.py:458
  3.5 1.5 %collective-permute-start = (bf16[1040,256]{1,0:T(8,128)(2,1)}, bf16[1040,256]{1,0:T(8,128)(2,1)S(1)}, u32[]{:S(2)}, u32[]{:S(2)}) collective-permute-start(bf16[1040,256]{1,0:T(8,128)(2,1)} %message.2.refs_0_), channel_id=1, source_target_pairs={{0,8},{8,0},{16,24},{24,16},{1,9},{9,1},{17,25},{25,17},{2,10},{10... | collective-permute-start | bytes 1597448 | tf_op jit(solution)/shard_map/ppermute | solution.py:458
  5.0 1.1 %copy-done.2 = bf16[1040,256]{1,0:T(8,128)(2,1)S(1)} copy-done((bf16[1040,256]{1,0:T(8,128)(2,1)S(1)}, bf16[1040,256]{1,0:T(8,128)(2,1)}, u32[]{:S(2)}) %copy-start.2) | copy-done | bytes 532504
  8.2 1.9 %grads.6 = (f32[3,256,512]{2,1,0:T(8,128)S(1)}, bf16[512,1024]{1,0:T(8,128)(2,1)S(1)}, bf16[512,512]{1,0:T(8,128)(2,1)S(1)}) custom-call(bf16[1040,256]{1,0:T(8,128)(2,1)S(1)} %copy-done.2, f32[256,512]{1,0:T(8,128)S(1)} %bitcast.3, f32[256,512]{1,0:T(8,128)S(1)} %bitcast.4, f32[512,256]{1,0:T(8,128)S(1)} %bitcast.5), custom_call_target="tpu_custom_call" | custom-call | tf_op jit(solution)/shard_map/grads/pallas_call | solution.py:416
  12.3 3.8 %collective-permute-done.1.refs_1_.refs_0_ = bf16[1040,256]{1,0:T(8,128)(2,1)S(1)} collective-permute-done((bf16[1040,256]{1,0:T(8,128)(2,1)}, bf16[1040,256]{1,0:T(8,128)(2,1)S(1)}, u32[]{:S(2)}, u32[]{:S(2)}) %collective-permute-start.1) | collective-permute-done | bytes 532512 | tf_op jit(solution)/shard_map/ppermute | solution.py:458
  16.1 1.6 %collective-permute-start.5 = (bf16[528,256]{1,0:T(8,128)(2,1)S(1)}, bf16[528,256]{1,0:T(8,128)(2,1)S(1)}, u32[]{:S(2)}, u32[]{:S(2)}) collective-permute-start(bf16[528,256]{1,0:T(8,128)(2,1)S(1)} %relay.4.refs_1_), channel_id=1, source_target_pairs={{0,8},{8,0},{16,24},{24,16},{1,9},{9,1},{17,25},{25,17},{2,10},{10... | collective-permute-start | bytes 811016 | tf_op jit(solution)/shard_map/ppermute | solution.py:458
  17.7 1.6 %collective-permute-start.4 = (bf16[512,256]{1,0:T(8,128)(2,1)S(1)}, bf16[512,256]{1,0:T(8,128)(2,1)S(1)}, u32[]{:S(2)}, u32[]{:S(2)}) collective-permute-start(bf16[512,256]{1,0:T(8,128)(2,1)S(1)} %relay.5), channel_id=1, source_target_pairs={{0,16},{8,24},{16,0},{24,8},{1,17},{9,25},{17,1},{25,9},{2,18},{10... | collective-permute-start | bytes 786440 | tf_op jit(solution)/shard_map/ppermute | solution.py:458
  19.3 3.4 %grads.7.refs_3_.refs_4_ = f32[3,256,512]{2,1,0:T(8,128)S(1)} custom-call(bf16[1040,256]{1,0:T(8,128)(2,1)S(1)} %collective-permute-done.refs_0_, bf16[1040,256]{1,0:T(8,128)(2,1)S(1)} %collective-permute-done.1.refs_1_.refs_0_, bf16[512,1024]{1,0:T(8,128)(2,1)S(1)} %get-tuple-element.25.refs_2_.refs_5_, ...), custom_call_target="tpu_custom_call" | custom-call | tf_op jit(solution)/shard_map/grads/pallas_call | solution.py:416
  23.3 1.2 %collective-permute-start.2 = (bf16[1040,256]{1,0:T(8,128)(2,1)S(1)}, bf16[1040,256]{1,0:T(8,128)(2,1)S(1)}, u32[]{:S(2)}, u32[]{:S(2)}) collective-permute-start(bf16[1040,256]{1,0:T(8,128)(2,1)S(1)} %message.3.refs_5_.refs_0_), channel_id=1, source_target_pairs={{0,8},{8,0},{16,24},{24,16},{1,9},{9,1},{17,25},{25,17},{2,10},{10... | collective-permute-start | bytes 1597448 | tf_op jit(solution)/shard_map/ppermute | solution.py:458
  24.6 1.8 %grads.8.refs_7_.refs_13_ = f32[3,256,512]{2,1,0:T(8,128)S(1)} custom-call(bf16[512,256]{1,0:T(8,128)(2,1)S(1)} %collective-permute-done.4.refs_0_.refs_1_.refs_3_, bf16[528,256]{1,0:T(8,128)(2,1)S(1)} %collective-permute-done.5.refs_1_.refs_2_.refs_4_, bf16[512,1024]{1,0:T(8,128)(2,1)S(1)} %get-tuple-element.25.refs_2_.refs_5_, ...), custom_call_target="tpu_custom_call" | custom-call | tf_op jit(solution)/shard_map/grads/pallas_call | solution.py:416
  26.4 7.9 %update.2 = (bf16[512,256]{1,0:T(8,128)(2,1)S(1)}, bf16[512,1024]{1,0:T(8,128)(2,1)S(1)}, bf16[512,512]{1,0:T(8,128)(2,1)S(1)}) custom-call(bf16[1040,256]{1,0:T(8,128)(2,1)S(1)} %collective-permute-done.refs_0_, bf16[512,256]{1,0:T(8,128)(2,1)S(1)} %collective-permute-done.4.refs_0_.refs_1_.refs_3_, ...), custom_call_target="tpu_custom_call" | custom-call | flops 30000001024 | tf_op jit(solution)/shard_map/update/pallas_call | solution.py:416
  34.4 1.8 %grads.9.refs_4_ = f32[3,256,512]{2,1,0:T(8,128)S(1)} custom-call(bf16[1040,256]{1,0:T(8,128)(2,1)S(1)} %message.3.refs_5_.refs_0_, bf16[512,1024]{1,0:T(8,128)(2,1)S(1)} %get-tuple-element.31.refs_1_.refs_2_.refs_5_, bf16[512,512]{1,0:T(8,128)(2,1)S(1)} %get-tuple-element.32.refs_2_.refs_3_.refs_6_, bf16[512,256]{1,0:T(8,128)(2,1)S(1)} %get-tuple-element.29.refs_3_.refs_0_), custom_call_target="tpu_custom_call" | custom-call | tf_op jit(solution)/shard_map/grads/pallas_call | solution.py:416
  38.3 1.2 %collective-permute-start.8 = (bf16[512,256]{1,0:T(8,128)(2,1)S(1)}, bf16[512,256]{1,0:T(8,128)(2,1)S(1)}, u32[]{:S(2)}, u32[]{:S(2)}) collective-permute-start(bf16[512,256]{1,0:T(8,128)(2,1)S(1)} %relay.7), channel_id=1, source_target_pairs={{0,16},{8,24},{16,0},{24,8},{1,17},{9,25},{17,1},{25,9},{2,18},{10... | collective-permute-start | bytes 786440 | tf_op jit(solution)/shard_map/ppermute | solution.py:458
  39.9 1.6 %collective-permute-start.15 = (bf16[512,256]{1,0:T(8,128)(2,1)S(1)}, bf16[512,256]{1,0:T(8,128)(2,1)S(1)}, u32[]{:S(2)}, u32[]{:S(2)}) collective-permute-start(bf16[512,256]{1,0:T(8,128)(2,1)S(1)} %get-tuple-element.44), channel_id=1, source_target_pairs={{0,2},{1,3},{2,0},{3,1},{4,6},{5,7},{6,4},{7,5},{8,10},{9,11},{10,... | collective-permute-start | bytes 786440 | tf_op jit(solution)/shard_map/ppermute | solution.py:458
  41.4 3.4 %grads.10.refs_4_ = f32[3,256,512]{2,1,0:T(8,128)S(1)} custom-call(bf16[1040,256]{1,0:T(8,128)(2,1)S(1)} %collective-permute-done.2.refs_0_, bf16[1040,256]{1,0:T(8,128)(2,1)S(1)} %collective-permute-done.3.refs_0_.refs_1_, bf16[512,1024]{1,0:T(8,128)(2,1)S(1)} %get-tuple-element.31.refs_1_.refs_2_.refs_5_, ...), custom_call_target="tpu_custom_call" | custom-call | tf_op jit(solution)/shard_map/grads/pallas_call | solution.py:416
  44.8 1.9 %collective-permute-done.8.refs_0_.refs_1_ = bf16[512,256]{1,0:T(8,128)(2,1)S(1)} collective-permute-done((bf16[512,256]{1,0:T(8,128)(2,1)S(1)}, bf16[512,256]{1,0:T(8,128)(2,1)S(1)}, u32[]{:S(2)}, u32[]{:S(2)}) %collective-permute-start.8) | collective-permute-done | bytes 262176 | tf_op jit(solution)/shard_map/ppermute | solution.py:458
  46.7 1.8 %grads.11.refs_2_.refs_7_ = f32[3,256,512]{2,1,0:T(8,128)S(1)} custom-call(bf16[512,256]{1,0:T(8,128)(2,1)S(1)} %collective-permute-done.8.refs_0_.refs_1_, bf16[528,256]{1,0:T(8,128)(2,1)S(1)} %collective-permute-done.9.refs_1_.refs_2_, bf16[512,1024]{1,0:T(8,128)(2,1)S(1)} %get-tuple-element.31.refs_1_.refs_2_.refs_5_, ...), custom_call_target="tpu_custom_call" | custom-call | tf_op jit(solution)/shard_map/grads/pallas_call | solution.py:416
  48.7 2.7 %collective-permute-start.16 = (bf16[512,256]{1,0:T(8,128)(2,1)S(1)}, bf16[512,256]{1,0:T(8,128)(2,1)S(1)}, u32[]{:S(2)}, u32[]{:S(2)}) collective-permute-start(bf16[512,256]{1,0:T(8,128)(2,1)S(1)} %add.1.refs_13_), channel_id=1, source_target_pairs={{0,4},{1,5},{2,6},{3,7},{4,0},{5,1},{6,2},{7,3},{8,12},{9,13},{10,... | collective-permute-start | bytes 786440 | tf_op jit(solution)/shard_map/ppermute | solution.py:458
  51.3 7.9 %update.3.refs_0_ = bf16[512,256]{1,0:T(8,128)(2,1)S(1)} custom-call(bf16[1040,256]{1,0:T(8,128)(2,1)S(1)} %collective-permute-done.2.refs_0_, bf16[512,256]{1,0:T(8,128)(2,1)S(1)} %collective-permute-done.8.refs_0_.refs_1_, bf16[528,256]{1,0:T(8,128)(2,1)S(1)} %collective-permute-done.9.refs_1_.refs_2_, ...), custom_call_target="tpu_custom_call" | custom-call | tf_op jit(solution)/shard_map/update/pallas_call | solution.py:416
  61.7 1.6 %collective-permute-start.13 = (bf16[512,256]{1,0:T(8,128)(2,1)S(1)}, bf16[512,256]{1,0:T(8,128)(2,1)S(1)}, u32[]{:S(2)}, u32[]{:S(2)}) collective-permute-start(bf16[512,256]{1,0:T(8,128)(2,1)S(1)} %get-tuple-element.42), channel_id=1, source_target_pairs={{0,6},{1,7},{2,4},{3,5},{4,2},{5,3},{6,0},{7,1},{8,14},{9,15},{10,... | collective-permute-start | bytes 786440 | tf_op jit(solution)/shard_map/ppermute | solution.py:458
  63.3 2.5 %collective-permute-start.14 = (bf16[512,256]{1,0:T(8,128)(2,1)S(1)}, bf16[512,256]{1,0:T(8,128)(2,1)S(1)}, u32[]{:S(2)}, u32[]{:S(2)}) collective-permute-start(bf16[512,256]{1,0:T(8,128)(2,1)S(1)} %get-tuple-element.43), channel_id=1, source_target_pairs={{0,2},{1,3},{2,0},{3,1},{4,6},{5,7},{6,4},{7,5},{8,10},{9,11},{10,... | collective-permute-start | bytes 786440 | tf_op jit(solution)/shard_map/ppermute | solution.py:458
  65.9 13.0 %collective-permute-done.12.refs_1_ = bf16[512,256]{1,0:T(8,128)(2,1)S(1)} collective-permute-done((bf16[512,256]{1,0:T(8,128)(2,1)S(1)}, bf16[512,256]{1,0:T(8,128)(2,1)S(1)}, u32[]{:S(2)}, u32[]{:S(2)}) %collective-permute-start.12) | collective-permute-done | bytes 262176 | tf_op jit(solution)/shard_map/ppermute | solution.py:458
  78.9 7.7 %collective-permute-done.13.refs_2_ = bf16[512,256]{1,0:T(8,128)(2,1)S(1)} collective-permute-done((bf16[512,256]{1,0:T(8,128)(2,1)S(1)}, bf16[512,256]{1,0:T(8,128)(2,1)S(1)}, u32[]{:S(2)}, u32[]{:S(2)}) %collective-permute-start.13) | collective-permute-done | bytes 262176 | tf_op jit(solution)/shard_map/ppermute | solution.py:458
  (52 shorter events, 11.1 us)
Async XLA Ops:
  0.0 5.0 %copy-start.5 = (f32[1,256,512]{2,1,0:T(8,128)S(1)}, f32[1,256,512]{2,1,0:T(8,128)}, u32[]{:S(2)}) copy-start(f32[1,256,512]{2,1,0:T(8,128)} %param.13) | copy-start | bytes 1572868
  0.0 10.1 %copy-start.4 = (bf16[256,2048]{1,0:T(8,128)(2,1)S(1)}, bf16[256,2048]{1,0:T(8,128)(2,1)}, u32[]{:S(2)}) copy-start(bf16[256,2048]{1,0:T(8,128)(2,1)} %refs_0_.3) | copy-start | bytes 3145732
  2.0 14.0 %collective-permute-start.1 = (bf16[1040,256]{1,0:T(8,128)(2,1)}, bf16[1040,256]{1,0:T(8,128)(2,1)S(1)}, u32[]{:S(2)}, u32[]{:S(2)}) collective-permute-start(bf16[1040,256]{1,0:T(8,128)(2,1)} %message.2.refs_0_), channel_id=1, source_target_pairs={{0,16},{8,24},{16,0},{24,8},{1,17},{9,25},{17,1},{25,9},{2,18},{10... | collective-permute-start | bytes 1597448 | tf_op jit(solution)/shard_map/ppermute | solution.py:458
  3.5 14.1 %collective-permute-start = (bf16[1040,256]{1,0:T(8,128)(2,1)}, bf16[1040,256]{1,0:T(8,128)(2,1)S(1)}, u32[]{:S(2)}, u32[]{:S(2)}) collective-permute-start(bf16[1040,256]{1,0:T(8,128)(2,1)} %message.2.refs_0_), channel_id=1, source_target_pairs={{0,8},{8,0},{16,24},{24,16},{1,9},{9,1},{17,25},{25,17},{2,10},{10... | collective-permute-start | bytes 1597448 | tf_op jit(solution)/shard_map/ppermute | solution.py:458
  5.0 1.1 %copy-start.2 = (bf16[1040,256]{1,0:T(8,128)(2,1)S(1)}, bf16[1040,256]{1,0:T(8,128)(2,1)}, u32[]{:S(2)}) copy-start(bf16[1040,256]{1,0:T(8,128)(2,1)} %message.2.refs_0_) | copy-start | bytes 1597444
  10.1 1.2 %copy-start.1 = (bf16[2,512,256]{2,1,0:T(8,128)(2,1)S(1)}, bf16[2,512,256]{2,1,0:T(8,128)(2,1)}, u32[]{:S(2)}) copy-start(bf16[2,512,256]{2,1,0:T(8,128)(2,1)} %refs_10_.3) | copy-start | bytes 1572868
  10.1 1.3 %copy-start.3 = (bf16[2,512,256]{2,1,0:T(8,128)(2,1)S(1)}, bf16[2,512,256]{2,1,0:T(8,128)(2,1)}, u32[]{:S(2)}) copy-start(bf16[2,512,256]{2,1,0:T(8,128)(2,1)} %refs_8_.3) | copy-start | bytes 1572868
  16.1 8.5 %collective-permute-start.5 = (bf16[528,256]{1,0:T(8,128)(2,1)S(1)}, bf16[528,256]{1,0:T(8,128)(2,1)S(1)}, u32[]{:S(2)}, u32[]{:S(2)}) collective-permute-start(bf16[528,256]{1,0:T(8,128)(2,1)S(1)} %relay.4.refs_1_), channel_id=1, source_target_pairs={{0,8},{8,0},{16,24},{24,16},{1,9},{9,1},{17,25},{25,17},{2,10},{10... | collective-permute-start | bytes 811016 | tf_op jit(solution)/shard_map/ppermute | solution.py:458
  17.7 7.0 %collective-permute-start.4 = (bf16[512,256]{1,0:T(8,128)(2,1)S(1)}, bf16[512,256]{1,0:T(8,128)(2,1)S(1)}, u32[]{:S(2)}, u32[]{:S(2)}) collective-permute-start(bf16[512,256]{1,0:T(8,128)(2,1)S(1)} %relay.5), channel_id=1, source_target_pairs={{0,16},{8,24},{16,0},{24,8},{1,17},{9,25},{17,1},{25,9},{2,18},{10... | collective-permute-start | bytes 786440 | tf_op jit(solution)/shard_map/ppermute | solution.py:458
  19.3 17.0 %collective-permute-start.7 = (bf16[256,1024]{1,0:T(8,128)(2,1)S(1)}, bf16[256,1024]{1,0:T(8,128)(2,1)S(1)}, u32[]{:S(2)}, u32[]{:S(2)}) collective-permute-start(bf16[256,1024]{1,0:T(8,128)(2,1)S(1)} %get-tuple-element.30), channel_id=1, source_target_pairs={{0,1},{1,0},{2,3},{3,2},{4,5},{5,4},{6,7},{7,6},{8,9},{9,8},{10,11... | collective-permute-start | bytes 1572872 | tf_op jit(solution)/shard_map/ppermute | solution.py:458
  19.3 3.4 %copy-start.8 = (f32[1,2,512]{2,1,0:T(2,128)S(1)}, f32[1,2,512]{2,1,0:T(2,128)}, u32[]{:S(2)}) copy-start(f32[1,2,512]{2,1,0:T(2,128)} %refs_2_.3) | copy-start | bytes 12292
  22.7 3.7 %copy-start.9 = (f32[1,256]{1,0:T(1,128)S(1)}, f32[1,256]{1,0:T(1,128)}, u32[]{:S(2)}) copy-start(f32[1,256]{1,0:T(1,128)} %refs_12_.3) | copy-start | bytes 3076
  22.7 14.6 %collective-permute-start.3 = (bf16[1040,256]{1,0:T(8,128)(2,1)S(1)}, bf16[1040,256]{1,0:T(8,128)(2,1)S(1)}, u32[]{:S(2)}, u32[]{:S(2)}) collective-permute-start(bf16[1040,256]{1,0:T(8,128)(2,1)S(1)} %message.3.refs_5_.refs_0_), channel_id=1, source_target_pairs={{0,16},{8,24},{16,0},{24,8},{1,17},{9,25},{17,1},{25,9},{2,18},{10... | collective-permute-start | bytes 1597448 | tf_op jit(solution)/shard_map/ppermute | solution.py:458
  23.3 14.9 %collective-permute-start.2 = (bf16[1040,256]{1,0:T(8,128)(2,1)S(1)}, bf16[1040,256]{1,0:T(8,128)(2,1)S(1)}, u32[]{:S(2)}, u32[]{:S(2)}) collective-permute-start(bf16[1040,256]{1,0:T(8,128)(2,1)S(1)} %message.3.refs_5_.refs_0_), channel_id=1, source_target_pairs={{0,8},{8,0},{16,24},{24,16},{1,9},{9,1},{17,25},{25,17},{2,10},{10... | collective-permute-start | bytes 1597448 | tf_op jit(solution)/shard_map/ppermute | solution.py:458
  34.3 1.9 %collective-permute-start.6 = (bf16[512,256]{1,0:T(8,128)(2,1)S(1)}, bf16[512,256]{1,0:T(8,128)(2,1)S(1)}, u32[]{:S(2)}, u32[]{:S(2)}) collective-permute-start(bf16[512,256]{1,0:T(8,128)(2,1)S(1)} %get-tuple-element.29.refs_3_.refs_0_), channel_id=1, source_target_pairs={{0,1},{1,0},{2,3},{3,2},{4,5},{5,4},{6,7},{7,6},{8,9},{9,8},{10,11... | collective-permute-start | bytes 786440 | tf_op jit(solution)/shard_map/ppermute | solution.py:458
  37.3 9.4 %collective-permute-start.9 = (bf16[528,256]{1,0:T(8,128)(2,1)S(1)}, bf16[528,256]{1,0:T(8,128)(2,1)S(1)}, u32[]{:S(2)}, u32[]{:S(2)}) collective-permute-start(bf16[528,256]{1,0:T(8,128)(2,1)S(1)} %relay.6.refs_1_), channel_id=1, source_target_pairs={{0,8},{8,0},{16,24},{24,16},{1,9},{9,1},{17,25},{25,17},{2,10},{10... | collective-permute-start | bytes 811016 | tf_op jit(solution)/shard_map/ppermute | solution.py:458
  38.3 8.5 %collective-permute-start.8 = (bf16[512,256]{1,0:T(8,128)(2,1)S(1)}, bf16[512,256]{1,0:T(8,128)(2,1)S(1)}, u32[]{:S(2)}, u32[]{:S(2)}) collective-permute-start(bf16[512,256]{1,0:T(8,128)(2,1)S(1)} %relay.7), channel_id=1, source_target_pairs={{0,16},{8,24},{16,0},{24,8},{1,17},{9,25},{17,1},{25,9},{2,18},{10... | collective-permute-start | bytes 786440 | tf_op jit(solution)/shard_map/ppermute | solution.py:458
  39.4 9.2 %collective-permute-start.10 = (bf16[512,256]{1,0:T(8,128)(2,1)S(1)}, bf16[512,256]{1,0:T(8,128)(2,1)S(1)}, u32[]{:S(2)}, u32[]{:S(2)}) collective-permute-start(bf16[512,256]{1,0:T(8,128)(2,1)S(1)} %get-tuple-element.35), channel_id=1, source_target_pairs={{0,2},{1,3},{2,0},{3,1},{4,6},{5,7},{6,4},{7,5},{8,10},{9,11},{10,... | collective-permute-start | bytes 786440 | tf_op jit(solution)/shard_map/ppermute | solution.py:458
  39.9 25.9 %collective-permute-start.15 = (bf16[512,256]{1,0:T(8,128)(2,1)S(1)}, bf16[512,256]{1,0:T(8,128)(2,1)S(1)}, u32[]{:S(2)}, u32[]{:S(2)}) collective-permute-start(bf16[512,256]{1,0:T(8,128)(2,1)S(1)} %get-tuple-element.44), channel_id=1, source_target_pairs={{0,2},{1,3},{2,0},{3,1},{4,6},{5,7},{6,4},{7,5},{8,10},{9,11},{10,... | collective-permute-start | bytes 786440 | tf_op jit(solution)/shard_map/ppermute | solution.py:458
  48.7 17.1 %collective-permute-start.16 = (bf16[512,256]{1,0:T(8,128)(2,1)S(1)}, bf16[512,256]{1,0:T(8,128)(2,1)S(1)}, u32[]{:S(2)}, u32[]{:S(2)}) collective-permute-start(bf16[512,256]{1,0:T(8,128)(2,1)S(1)} %add.1.refs_13_), channel_id=1, source_target_pairs={{0,4},{1,5},{2,6},{3,7},{4,0},{5,1},{6,2},{7,3},{8,12},{9,13},{10,... | collective-permute-start | bytes 786440 | tf_op jit(solution)/shard_map/ppermute | solution.py:458
  59.2 1.6 %collective-permute-start.11 = (bf16[512,256]{1,0:T(8,128)(2,1)S(1)}, bf16[512,256]{1,0:T(8,128)(2,1)S(1)}, u32[]{:S(2)}, u32[]{:S(2)}) collective-permute-start(bf16[512,256]{1,0:T(8,128)(2,1)S(1)} %update.3.refs_0_), channel_id=1, source_target_pairs={{0,1},{1,0},{2,3},{3,2},{4,5},{5,4},{6,7},{7,6},{8,9},{9,8},{10,11... | collective-permute-start | bytes 786440 | tf_op jit(solution)/shard_map/ppermute | solution.py:458
  61.3 17.5 %collective-permute-start.12 = (bf16[512,256]{1,0:T(8,128)(2,1)S(1)}, bf16[512,256]{1,0:T(8,128)(2,1)S(1)}, u32[]{:S(2)}, u32[]{:S(2)}) collective-permute-start(bf16[512,256]{1,0:T(8,128)(2,1)S(1)} %get-tuple-element.41), channel_id=1, source_target_pairs={{0,4},{1,5},{2,6},{3,7},{4,0},{5,1},{6,2},{7,3},{8,12},{9,13},{10,... | collective-permute-start | bytes 786440 | tf_op jit(solution)/shard_map/ppermute | solution.py:458
  61.7 24.8 %collective-permute-start.13 = (bf16[512,256]{1,0:T(8,128)(2,1)S(1)}, bf16[512,256]{1,0:T(8,128)(2,1)S(1)}, u32[]{:S(2)}, u32[]{:S(2)}) collective-permute-start(bf16[512,256]{1,0:T(8,128)(2,1)S(1)} %get-tuple-element.42), channel_id=1, source_target_pairs={{0,6},{1,7},{2,4},{3,5},{4,2},{5,3},{6,0},{7,1},{8,14},{9,15},{10,... | collective-permute-start | bytes 786440 | tf_op jit(solution)/shard_map/ppermute | solution.py:458
  63.3 23.2 %collective-permute-start.14 = (bf16[512,256]{1,0:T(8,128)(2,1)S(1)}, bf16[512,256]{1,0:T(8,128)(2,1)S(1)}, u32[]{:S(2)}, u32[]{:S(2)}) collective-permute-start(bf16[512,256]{1,0:T(8,128)(2,1)S(1)} %get-tuple-element.43), channel_id=1, source_target_pairs={{0,2},{1,3},{2,0},{3,1},{4,6},{5,7},{6,4},{7,5},{8,10},{9,11},{10,... | collective-permute-start | bytes 786440 | tf_op jit(solution)/shard_map/ppermute | solution.py:458
  (3 other events, 3.1 us)

commit v3 on v2

--- a/solution.py
+++ b/solution.py
@@ -483,7 +483,7 @@
         [shape((rows, width), f32)] + [shape((rows, width), bf16)] * (chips - 1),
         [other, other_proj, *parts], "other_part",
     )
-    order = [*range(2, chips), 1]
+    order = [2, 1, *range(3, chips)]
     return [kept] + [to_chip(sent[step - 1], step) for step in order]
 
 

time: 87.8 us -> 87.8 us (level)
  starting transfers between devices: 19.2 us -> 18.3 us
  waiting for transfers between devices: 28 us -> 28.9 us
    ppermute x17, starting transfers between devices: 19.2 us -> 18.3 us  [shifted(): return lax.ppermute(value, axis, [(at, at ^ step) for at in range(count)])]
    ppermute x17, waiting for transfers between devices: 28 us -> 28.9 us  [shifted(): return lax.ppermute(value, axis, [(at, at ^ step) for at in range(count)])]
  transfers between devices with their start and end apart: 17 -> 17, of which waited for: 8 -> 9; matrix products, arithmetic and copies ran while one was open for 0% -> 0% of each run, Pallas kernels for 37% -> 37%
where the time goes in v3:
time: 87.8 us; the launch traced here: 87.5 us
  Pallas kernels  35.6 us (41%)
  waiting for transfers between devices  28.9 us (33%)
  starting transfers between devices  18.3 us (21%)
  local copies, waits for them, and re-layouts  4.34 us (5%)
    pallas_call x21, Pallas kernels, call(): pl.pallas_call(reading, out_shape=out_shape, in_specs=[VMEM] * count + [A...  33.6 us
    ppermute x17, waiting for transfers between devices, shifted(): return lax.ppermute(value, axis, [(at, at ^ step) for at in range(count)])  28.9 us
    ppermute x17, starting transfers between devices, shifted(): return lax.ppermute(value, axis, [(at, at ^ step) for at in range(count)])  18.3 us
    unnamed x20, local copies, waits for them, and re-layouts  4.34 us
    pallas_call x1, Pallas kernels, first_message(): pl.pallas_call(functools.partial(message_kernel, 0), out_shape=shape(dims...  2.01 us
  transfers between devices with their start and end apart: 17, of which 9 were waited for; matrix products, arithmetic and copies ran while one was open for 0% of the time, Pallas kernels for 37%

profile of v3, /device:TPU:8, one launch (start us, length us, event | category | flops | bytes accessed | tf_op | source)
XLA Modules:
  0.0 87.5 jit_solution(17636445472537003169)
XLA Ops:
  0.0 2.0 %message.2.refs_0_ = bf16[1040,256]{1,0:T(8,128)(2,1)} custom-call(bf16[2,512,256]{2,1,0:T(8,128)(2,1)} %refs_9_.3, bf16[2,512,256]{2,1,0:T(8,128)(2,1)} %refs_10_.3, f32[1,2,512]{2,1,0:T(2,128)} %refs_2_.3), custom_call_target="tpu_custom_call" | custom-call | tf_op jit(solution)/shard_map/message/pallas_call | solution.py:436
  2.0 1.5 %collective-permute-start.1 = (bf16[1040,256]{1,0:T(8,128)(2,1)}, bf16[1040,256]{1,0:T(8,128)(2,1)S(1)}, u32[]{:S(2)}, u32[]{:S(2)}) collective-permute-start(bf16[1040,256]{1,0:T(8,128)(2,1)} %message.2.refs_0_), channel_id=1, source_target_pairs={{0,16},{8,24},{16,0},{24,8},{1,17},{9,25},{17,1},{25,9},{2,18},{10... | collective-permute-start | bytes 1597448 | tf_op jit(solution)/shard_map/ppermute | solution.py:458
  3.5 1.5 %collective-permute-start = (bf16[1040,256]{1,0:T(8,128)(2,1)}, bf16[1040,256]{1,0:T(8,128)(2,1)S(1)}, u32[]{:S(2)}, u32[]{:S(2)}) collective-permute-start(bf16[1040,256]{1,0:T(8,128)(2,1)} %message.2.refs_0_), channel_id=1, source_target_pairs={{0,8},{8,0},{16,24},{24,16},{1,9},{9,1},{17,25},{25,17},{2,10},{10... | collective-permute-start | bytes 1597448 | tf_op jit(solution)/shard_map/ppermute | solution.py:458
  5.0 1.1 %copy-done.2 = bf16[1040,256]{1,0:T(8,128)(2,1)S(1)} copy-done((bf16[1040,256]{1,0:T(8,128)(2,1)S(1)}, bf16[1040,256]{1,0:T(8,128)(2,1)}, u32[]{:S(2)}) %copy-start.2) | copy-done | bytes 532504
  8.2 1.9 %grads.6 = (f32[3,256,512]{2,1,0:T(8,128)S(1)}, bf16[512,1024]{1,0:T(8,128)(2,1)S(1)}, bf16[512,512]{1,0:T(8,128)(2,1)S(1)}) custom-call(bf16[1040,256]{1,0:T(8,128)(2,1)S(1)} %copy-done.2, f32[256,512]{1,0:T(8,128)S(1)} %bitcast.3, f32[256,512]{1,0:T(8,128)S(1)} %bitcast.4, f32[512,256]{1,0:T(8,128)S(1)} %bitcast.5), custom_call_target="tpu_custom_call" | custom-call | tf_op jit(solution)/shard_map/grads/pallas_call | solution.py:416
  12.3 3.8 %collective-permute-done.1.refs_1_.refs_0_ = bf16[1040,256]{1,0:T(8,128)(2,1)S(1)} collective-permute-done((bf16[1040,256]{1,0:T(8,128)(2,1)}, bf16[1040,256]{1,0:T(8,128)(2,1)S(1)}, u32[]{:S(2)}, u32[]{:S(2)}) %collective-permute-start.1) | collective-permute-done | bytes 532512 | tf_op jit(solution)/shard_map/ppermute | solution.py:458
  16.1 1.6 %collective-permute-start.5 = (bf16[528,256]{1,0:T(8,128)(2,1)S(1)}, bf16[528,256]{1,0:T(8,128)(2,1)S(1)}, u32[]{:S(2)}, u32[]{:S(2)}) collective-permute-start(bf16[528,256]{1,0:T(8,128)(2,1)S(1)} %relay.4.refs_1_), channel_id=1, source_target_pairs={{0,8},{8,0},{16,24},{24,16},{1,9},{9,1},{17,25},{25,17},{2,10},{10... | collective-permute-start | bytes 811016 | tf_op jit(solution)/shard_map/ppermute | solution.py:458
  17.7 1.6 %collective-permute-start.4 = (bf16[512,256]{1,0:T(8,128)(2,1)S(1)}, bf16[512,256]{1,0:T(8,128)(2,1)S(1)}, u32[]{:S(2)}, u32[]{:S(2)}) collective-permute-start(bf16[512,256]{1,0:T(8,128)(2,1)S(1)} %relay.5), channel_id=1, source_target_pairs={{0,16},{8,24},{16,0},{24,8},{1,17},{9,25},{17,1},{25,9},{2,18},{10... | collective-permute-start | bytes 786440 | tf_op jit(solution)/shard_map/ppermute | solution.py:458
  19.3 3.4 %grads.7.refs_3_.refs_4_ = f32[3,256,512]{2,1,0:T(8,128)S(1)} custom-call(bf16[1040,256]{1,0:T(8,128)(2,1)S(1)} %collective-permute-done.refs_0_, bf16[1040,256]{1,0:T(8,128)(2,1)S(1)} %collective-permute-done.1.refs_1_.refs_0_, bf16[512,1024]{1,0:T(8,128)(2,1)S(1)} %get-tuple-element.25.refs_2_.refs_5_, ...), custom_call_target="tpu_custom_call" | custom-call | tf_op jit(solution)/shard_map/grads/pallas_call | solution.py:416
  23.3 1.2 %collective-permute-start.2 = (bf16[1040,256]{1,0:T(8,128)(2,1)S(1)}, bf16[1040,256]{1,0:T(8,128)(2,1)S(1)}, u32[]{:S(2)}, u32[]{:S(2)}) collective-permute-start(bf16[1040,256]{1,0:T(8,128)(2,1)S(1)} %message.3.refs_5_.refs_0_), channel_id=1, source_target_pairs={{0,8},{8,0},{16,24},{24,16},{1,9},{9,1},{17,25},{25,17},{2,10},{10... | collective-permute-start | bytes 1597448 | tf_op jit(solution)/shard_map/ppermute | solution.py:458
  24.6 1.8 %grads.8.refs_7_.refs_13_ = f32[3,256,512]{2,1,0:T(8,128)S(1)} custom-call(bf16[512,256]{1,0:T(8,128)(2,1)S(1)} %collective-permute-done.4.refs_0_.refs_1_.refs_3_, bf16[528,256]{1,0:T(8,128)(2,1)S(1)} %collective-permute-done.5.refs_1_.refs_2_.refs_4_, bf16[512,1024]{1,0:T(8,128)(2,1)S(1)} %get-tuple-element.25.refs_2_.refs_5_, ...), custom_call_target="tpu_custom_call" | custom-call | tf_op jit(solution)/shard_map/grads/pallas_call | solution.py:416
  26.4 7.9 %update.2 = (bf16[512,256]{1,0:T(8,128)(2,1)S(1)}, bf16[512,1024]{1,0:T(8,128)(2,1)S(1)}, bf16[512,512]{1,0:T(8,128)(2,1)S(1)}) custom-call(bf16[1040,256]{1,0:T(8,128)(2,1)S(1)} %collective-permute-done.refs_0_, bf16[512,256]{1,0:T(8,128)(2,1)S(1)} %collective-permute-done.4.refs_0_.refs_1_.refs_3_, ...), custom_call_target="tpu_custom_call" | custom-call | flops 30000001024 | tf_op jit(solution)/shard_map/update/pallas_call | solution.py:416
  34.4 1.8 %grads.9.refs_4_ = f32[3,256,512]{2,1,0:T(8,128)S(1)} custom-call(bf16[1040,256]{1,0:T(8,128)(2,1)S(1)} %message.3.refs_5_.refs_0_, bf16[512,1024]{1,0:T(8,128)(2,1)S(1)} %get-tuple-element.31.refs_1_.refs_2_.refs_5_, bf16[512,512]{1,0:T(8,128)(2,1)S(1)} %get-tuple-element.32.refs_2_.refs_3_.refs_6_, bf16[512,256]{1,0:T(8,128)(2,1)S(1)} %get-tuple-element.29.refs_3_.refs_0_), custom_call_target="tpu_custom_call" | custom-call | tf_op jit(solution)/shard_map/grads/pallas_call | solution.py:416
  38.3 1.2 %collective-permute-start.8 = (bf16[512,256]{1,0:T(8,128)(2,1)S(1)}, bf16[512,256]{1,0:T(8,128)(2,1)S(1)}, u32[]{:S(2)}, u32[]{:S(2)}) collective-permute-start(bf16[512,256]{1,0:T(8,128)(2,1)S(1)} %relay.7), channel_id=1, source_target_pairs={{0,16},{8,24},{16,0},{24,8},{1,17},{9,25},{17,1},{25,9},{2,18},{10... | collective-permute-start | bytes 786440 | tf_op jit(solution)/shard_map/ppermute | solution.py:458
  39.9 1.6 %collective-permute-start.15 = (bf16[512,256]{1,0:T(8,128)(2,1)S(1)}, bf16[512,256]{1,0:T(8,128)(2,1)S(1)}, u32[]{:S(2)}, u32[]{:S(2)}) collective-permute-start(bf16[512,256]{1,0:T(8,128)(2,1)S(1)} %get-tuple-element.44), channel_id=1, source_target_pairs={{0,2},{1,3},{2,0},{3,1},{4,6},{5,7},{6,4},{7,5},{8,10},{9,11},{10,... | collective-permute-start | bytes 786440 | tf_op jit(solution)/shard_map/ppermute | solution.py:458
  41.4 3.4 %grads.10.refs_4_ = f32[3,256,512]{2,1,0:T(8,128)S(1)} custom-call(bf16[1040,256]{1,0:T(8,128)(2,1)S(1)} %collective-permute-done.2.refs_0_, bf16[1040,256]{1,0:T(8,128)(2,1)S(1)} %collective-permute-done.3.refs_0_.refs_1_, bf16[512,1024]{1,0:T(8,128)(2,1)S(1)} %get-tuple-element.31.refs_1_.refs_2_.refs_5_, ...), custom_call_target="tpu_custom_call" | custom-call | tf_op jit(solution)/shard_map/grads/pallas_call | solution.py:416
  44.8 1.9 %collective-permute-done.8.refs_0_.refs_1_ = bf16[512,256]{1,0:T(8,128)(2,1)S(1)} collective-permute-done((bf16[512,256]{1,0:T(8,128)(2,1)S(1)}, bf16[512,256]{1,0:T(8,128)(2,1)S(1)}, u32[]{:S(2)}, u32[]{:S(2)}) %collective-permute-start.8) | collective-permute-done | bytes 262176 | tf_op jit(solution)/shard_map/ppermute | solution.py:458
  46.7 1.8 %grads.11.refs_2_.refs_7_ = f32[3,256,512]{2,1,0:T(8,128)S(1)} custom-call(bf16[512,256]{1,0:T(8,128)(2,1)S(1)} %collective-permute-done.8.refs_0_.refs_1_, bf16[528,256]{1,0:T(8,128)(2,1)S(1)} %collective-permute-done.9.refs_1_.refs_2_, bf16[512,1024]{1,0:T(8,128)(2,1)S(1)} %get-tuple-element.31.refs_1_.refs_2_.refs_5_, ...), custom_call_target="tpu_custom_call" | custom-call | tf_op jit(solution)/shard_map/grads/pallas_call | solution.py:416
  48.7 2.7 %collective-permute-start.16 = (bf16[512,256]{1,0:T(8,128)(2,1)S(1)}, bf16[512,256]{1,0:T(8,128)(2,1)S(1)}, u32[]{:S(2)}, u32[]{:S(2)}) collective-permute-start(bf16[512,256]{1,0:T(8,128)(2,1)S(1)} %add.1.refs_13_), channel_id=1, source_target_pairs={{0,4},{1,5},{2,6},{3,7},{4,0},{5,1},{6,2},{7,3},{8,12},{9,13},{10,... | collective-permute-start | bytes 786440 | tf_op jit(solution)/shard_map/ppermute | solution.py:458
  51.3 7.9 %update.3.refs_0_ = bf16[512,256]{1,0:T(8,128)(2,1)S(1)} custom-call(bf16[1040,256]{1,0:T(8,128)(2,1)S(1)} %collective-permute-done.2.refs_0_, bf16[512,256]{1,0:T(8,128)(2,1)S(1)} %collective-permute-done.8.refs_0_.refs_1_, bf16[528,256]{1,0:T(8,128)(2,1)S(1)} %collective-permute-done.9.refs_1_.refs_2_, ...), custom_call_target="tpu_custom_call" | custom-call | tf_op jit(solution)/shard_map/update/pallas_call | solution.py:416
  59.8 1.1 %collective-permute-done.11.refs_0_ = bf16[512,256]{1,0:T(8,128)(2,1)S(1)} collective-permute-done((bf16[512,256]{1,0:T(8,128)(2,1)S(1)}, bf16[512,256]{1,0:T(8,128)(2,1)S(1)}, u32[]{:S(2)}, u32[]{:S(2)}) %collective-permute-start.11) | collective-permute-done | bytes 262176 | tf_op jit(solution)/shard_map/ppermute | solution.py:458
  62.2 2.7 %collective-permute-start.14 = (bf16[512,256]{1,0:T(8,128)(2,1)S(1)}, bf16[512,256]{1,0:T(8,128)(2,1)S(1)}, u32[]{:S(2)}, u32[]{:S(2)}) collective-permute-start(bf16[512,256]{1,0:T(8,128)(2,1)S(1)} %get-tuple-element.43), channel_id=1, source_target_pairs={{0,6},{1,7},{2,4},{3,5},{4,2},{5,3},{6,0},{7,1},{8,14},{9,15},{10,... | collective-permute-start | bytes 786440 | tf_op jit(solution)/shard_map/ppermute | solution.py:458
  65.0 9.0 %collective-permute-done.12.refs_1_ = bf16[512,256]{1,0:T(8,128)(2,1)S(1)} collective-permute-done((bf16[512,256]{1,0:T(8,128)(2,1)S(1)}, bf16[512,256]{1,0:T(8,128)(2,1)S(1)}, u32[]{:S(2)}, u32[]{:S(2)}) %collective-permute-start.12) | collective-permute-done | bytes 262176 | tf_op jit(solution)/shard_map/ppermute | solution.py:458
  75.0 11.6 %collective-permute-done.14.refs_3_ = bf16[512,256]{1,0:T(8,128)(2,1)S(1)} collective-permute-done((bf16[512,256]{1,0:T(8,128)(2,1)S(1)}, bf16[512,256]{1,0:T(8,128)(2,1)S(1)}, u32[]{:S(2)}, u32[]{:S(2)}) %collective-permute-start.14) | collective-permute-done | bytes 262176 | tf_op jit(solution)/shard_map/ppermute | solution.py:458
  (52 shorter events, 11.5 us)
Async XLA Ops:
  0.0 5.0 %copy-start.5 = (f32[1,256,512]{2,1,0:T(8,128)S(1)}, f32[1,256,512]{2,1,0:T(8,128)}, u32[]{:S(2)}) copy-start(f32[1,256,512]{2,1,0:T(8,128)} %param.13) | copy-start | bytes 1572868
  0.0 10.1 %copy-start.4 = (bf16[256,2048]{1,0:T(8,128)(2,1)S(1)}, bf16[256,2048]{1,0:T(8,128)(2,1)}, u32[]{:S(2)}) copy-start(bf16[256,2048]{1,0:T(8,128)(2,1)} %refs_0_.3) | copy-start | bytes 3145732
  2.0 14.0 %collective-permute-start.1 = (bf16[1040,256]{1,0:T(8,128)(2,1)}, bf16[1040,256]{1,0:T(8,128)(2,1)S(1)}, u32[]{:S(2)}, u32[]{:S(2)}) collective-permute-start(bf16[1040,256]{1,0:T(8,128)(2,1)} %message.2.refs_0_), channel_id=1, source_target_pairs={{0,16},{8,24},{16,0},{24,8},{1,17},{9,25},{17,1},{25,9},{2,18},{10... | collective-permute-start | bytes 1597448 | tf_op jit(solution)/shard_map/ppermute | solution.py:458
  3.5 14.1 %collective-permute-start = (bf16[1040,256]{1,0:T(8,128)(2,1)}, bf16[1040,256]{1,0:T(8,128)(2,1)S(1)}, u32[]{:S(2)}, u32[]{:S(2)}) collective-permute-start(bf16[1040,256]{1,0:T(8,128)(2,1)} %message.2.refs_0_), channel_id=1, source_target_pairs={{0,8},{8,0},{16,24},{24,16},{1,9},{9,1},{17,25},{25,17},{2,10},{10... | collective-permute-start | bytes 1597448 | tf_op jit(solution)/shard_map/ppermute | solution.py:458
  5.0 1.1 %copy-start.2 = (bf16[1040,256]{1,0:T(8,128)(2,1)S(1)}, bf16[1040,256]{1,0:T(8,128)(2,1)}, u32[]{:S(2)}) copy-start(bf16[1040,256]{1,0:T(8,128)(2,1)} %message.2.refs_0_) | copy-start | bytes 1597444
  10.1 1.2 %copy-start.1 = (bf16[2,512,256]{2,1,0:T(8,128)(2,1)S(1)}, bf16[2,512,256]{2,1,0:T(8,128)(2,1)}, u32[]{:S(2)}) copy-start(bf16[2,512,256]{2,1,0:T(8,128)(2,1)} %refs_10_.3) | copy-start | bytes 1572868
  10.1 1.3 %copy-start.3 = (bf16[2,512,256]{2,1,0:T(8,128)(2,1)S(1)}, bf16[2,512,256]{2,1,0:T(8,128)(2,1)}, u32[]{:S(2)}) copy-start(bf16[2,512,256]{2,1,0:T(8,128)(2,1)} %refs_8_.3) | copy-start | bytes 1572868
  16.1 8.5 %collective-permute-start.5 = (bf16[528,256]{1,0:T(8,128)(2,1)S(1)}, bf16[528,256]{1,0:T(8,128)(2,1)S(1)}, u32[]{:S(2)}, u32[]{:S(2)}) collective-permute-start(bf16[528,256]{1,0:T(8,128)(2,1)S(1)} %relay.4.refs_1_), channel_id=1, source_target_pairs={{0,8},{8,0},{16,24},{24,16},{1,9},{9,1},{17,25},{25,17},{2,10},{10... | collective-permute-start | bytes 811016 | tf_op jit(solution)/shard_map/ppermute | solution.py:458
  17.7 7.0 %collective-permute-start.4 = (bf16[512,256]{1,0:T(8,128)(2,1)S(1)}, bf16[512,256]{1,0:T(8,128)(2,1)S(1)}, u32[]{:S(2)}, u32[]{:S(2)}) collective-permute-start(bf16[512,256]{1,0:T(8,128)(2,1)S(1)} %relay.5), channel_id=1, source_target_pairs={{0,16},{8,24},{16,0},{24,8},{1,17},{9,25},{17,1},{25,9},{2,18},{10... | collective-permute-start | bytes 786440 | tf_op jit(solution)/shard_map/ppermute | solution.py:458
  19.3 17.0 %collective-permute-start.7 = (bf16[256,1024]{1,0:T(8,128)(2,1)S(1)}, bf16[256,1024]{1,0:T(8,128)(2,1)S(1)}, u32[]{:S(2)}, u32[]{:S(2)}) collective-permute-start(bf16[256,1024]{1,0:T(8,128)(2,1)S(1)} %get-tuple-element.30), channel_id=1, source_target_pairs={{0,1},{1,0},{2,3},{3,2},{4,5},{5,4},{6,7},{7,6},{8,9},{9,8},{10,11... | collective-permute-start | bytes 1572872 | tf_op jit(solution)/shard_map/ppermute | solution.py:458
  19.3 3.4 %copy-start.8 = (f32[1,2,512]{2,1,0:T(2,128)S(1)}, f32[1,2,512]{2,1,0:T(2,128)}, u32[]{:S(2)}) copy-start(f32[1,2,512]{2,1,0:T(2,128)} %refs_2_.3) | copy-start | bytes 12292
  22.7 3.7 %copy-start.9 = (f32[1,256]{1,0:T(1,128)S(1)}, f32[1,256]{1,0:T(1,128)}, u32[]{:S(2)}) copy-start(f32[1,256]{1,0:T(1,128)} %refs_12_.3) | copy-start | bytes 3076
  22.7 14.6 %collective-permute-start.3 = (bf16[1040,256]{1,0:T(8,128)(2,1)S(1)}, bf16[1040,256]{1,0:T(8,128)(2,1)S(1)}, u32[]{:S(2)}, u32[]{:S(2)}) collective-permute-start(bf16[1040,256]{1,0:T(8,128)(2,1)S(1)} %message.3.refs_5_.refs_0_), channel_id=1, source_target_pairs={{0,16},{8,24},{16,0},{24,8},{1,17},{9,25},{17,1},{25,9},{2,18},{10... | collective-permute-start | bytes 1597448 | tf_op jit(solution)/shard_map/ppermute | solution.py:458
  23.3 14.9 %collective-permute-start.2 = (bf16[1040,256]{1,0:T(8,128)(2,1)S(1)}, bf16[1040,256]{1,0:T(8,128)(2,1)S(1)}, u32[]{:S(2)}, u32[]{:S(2)}) collective-permute-start(bf16[1040,256]{1,0:T(8,128)(2,1)S(1)} %message.3.refs_5_.refs_0_), channel_id=1, source_target_pairs={{0,8},{8,0},{16,24},{24,16},{1,9},{9,1},{17,25},{25,17},{2,10},{10... | collective-permute-start | bytes 1597448 | tf_op jit(solution)/shard_map/ppermute | solution.py:458
  34.3 1.9 %collective-permute-start.6 = (bf16[512,256]{1,0:T(8,128)(2,1)S(1)}, bf16[512,256]{1,0:T(8,128)(2,1)S(1)}, u32[]{:S(2)}, u32[]{:S(2)}) collective-permute-start(bf16[512,256]{1,0:T(8,128)(2,1)S(1)} %get-tuple-element.29.refs_3_.refs_0_), channel_id=1, source_target_pairs={{0,1},{1,0},{2,3},{3,2},{4,5},{5,4},{6,7},{7,6},{8,9},{9,8},{10,11... | collective-permute-start | bytes 786440 | tf_op jit(solution)/shard_map/ppermute | solution.py:458
  37.3 9.4 %collective-permute-start.9 = (bf16[528,256]{1,0:T(8,128)(2,1)S(1)}, bf16[528,256]{1,0:T(8,128)(2,1)S(1)}, u32[]{:S(2)}, u32[]{:S(2)}) collective-permute-start(bf16[528,256]{1,0:T(8,128)(2,1)S(1)} %relay.6.refs_1_), channel_id=1, source_target_pairs={{0,8},{8,0},{16,24},{24,16},{1,9},{9,1},{17,25},{25,17},{2,10},{10... | collective-permute-start | bytes 811016 | tf_op jit(solution)/shard_map/ppermute | solution.py:458
  38.3 8.5 %collective-permute-start.8 = (bf16[512,256]{1,0:T(8,128)(2,1)S(1)}, bf16[512,256]{1,0:T(8,128)(2,1)S(1)}, u32[]{:S(2)}, u32[]{:S(2)}) collective-permute-start(bf16[512,256]{1,0:T(8,128)(2,1)S(1)} %relay.7), channel_id=1, source_target_pairs={{0,16},{8,24},{16,0},{24,8},{1,17},{9,25},{17,1},{25,9},{2,18},{10... | collective-permute-start | bytes 786440 | tf_op jit(solution)/shard_map/ppermute | solution.py:458
  39.4 9.2 %collective-permute-start.10 = (bf16[512,256]{1,0:T(8,128)(2,1)S(1)}, bf16[512,256]{1,0:T(8,128)(2,1)S(1)}, u32[]{:S(2)}, u32[]{:S(2)}) collective-permute-start(bf16[512,256]{1,0:T(8,128)(2,1)S(1)} %get-tuple-element.35), channel_id=1, source_target_pairs={{0,2},{1,3},{2,0},{3,1},{4,6},{5,7},{6,4},{7,5},{8,10},{9,11},{10,... | collective-permute-start | bytes 786440 | tf_op jit(solution)/shard_map/ppermute | solution.py:458
  39.9 25.0 %collective-permute-start.15 = (bf16[512,256]{1,0:T(8,128)(2,1)S(1)}, bf16[512,256]{1,0:T(8,128)(2,1)S(1)}, u32[]{:S(2)}, u32[]{:S(2)}) collective-permute-start(bf16[512,256]{1,0:T(8,128)(2,1)S(1)} %get-tuple-element.44), channel_id=1, source_target_pairs={{0,2},{1,3},{2,0},{3,1},{4,6},{5,7},{6,4},{7,5},{8,10},{9,11},{10,... | collective-permute-start | bytes 786440 | tf_op jit(solution)/shard_map/ppermute | solution.py:458
  48.7 16.2 %collective-permute-start.16 = (bf16[512,256]{1,0:T(8,128)(2,1)S(1)}, bf16[512,256]{1,0:T(8,128)(2,1)S(1)}, u32[]{:S(2)}, u32[]{:S(2)}) collective-permute-start(bf16[512,256]{1,0:T(8,128)(2,1)S(1)} %add.1.refs_13_), channel_id=1, source_target_pairs={{0,4},{1,5},{2,6},{3,7},{4,0},{5,1},{6,2},{7,3},{8,12},{9,13},{10,... | collective-permute-start | bytes 786440 | tf_op jit(solution)/shard_map/ppermute | solution.py:458
  59.2 1.6 %collective-permute-start.11 = (bf16[512,256]{1,0:T(8,128)(2,1)S(1)}, bf16[512,256]{1,0:T(8,128)(2,1)S(1)}, u32[]{:S(2)}, u32[]{:S(2)}) collective-permute-start(bf16[512,256]{1,0:T(8,128)(2,1)S(1)} %update.3.refs_0_), channel_id=1, source_target_pairs={{0,1},{1,0},{2,3},{3,2},{4,5},{5,4},{6,7},{7,6},{8,9},{9,8},{10,11... | collective-permute-start | bytes 786440 | tf_op jit(solution)/shard_map/ppermute | solution.py:458
  61.3 12.7 %collective-permute-start.12 = (bf16[512,256]{1,0:T(8,128)(2,1)S(1)}, bf16[512,256]{1,0:T(8,128)(2,1)S(1)}, u32[]{:S(2)}, u32[]{:S(2)}) collective-permute-start(bf16[512,256]{1,0:T(8,128)(2,1)S(1)} %get-tuple-element.41), channel_id=1, source_target_pairs={{0,4},{1,5},{2,6},{3,7},{4,0},{5,1},{6,2},{7,3},{8,12},{9,13},{10,... | collective-permute-start | bytes 786440 | tf_op jit(solution)/shard_map/ppermute | solution.py:458
  61.7 13.2 %collective-permute-start.13 = (bf16[512,256]{1,0:T(8,128)(2,1)S(1)}, bf16[512,256]{1,0:T(8,128)(2,1)S(1)}, u32[]{:S(2)}, u32[]{:S(2)}) collective-permute-start(bf16[512,256]{1,0:T(8,128)(2,1)S(1)} %get-tuple-element.42), channel_id=1, source_target_pairs={{0,2},{1,3},{2,0},{3,1},{4,6},{5,7},{6,4},{7,5},{8,10},{9,11},{10,... | collective-permute-start | bytes 786440 | tf_op jit(solution)/shard_map/ppermute | solution.py:458
  62.2 24.3 %collective-permute-start.14 = (bf16[512,256]{1,0:T(8,128)(2,1)S(1)}, bf16[512,256]{1,0:T(8,128)(2,1)S(1)}, u32[]{:S(2)}, u32[]{:S(2)}) collective-permute-start(bf16[512,256]{1,0:T(8,128)(2,1)S(1)} %get-tuple-element.43), channel_id=1, source_target_pairs={{0,6},{1,7},{2,4},{3,5},{4,2},{5,3},{6,0},{7,1},{8,14},{9,15},{10,... | collective-permute-start | bytes 786440 | tf_op jit(solution)/shard_map/ppermute | solution.py:458
  (3 other events, 3.1 us)

commit v4 on v3

--- a/solution.py
+++ b/solution.py
@@ -150,13 +150,17 @@
 
 
 def gram_of(parts):
-    whole = mm(parts[0], parts[0], NT)
-    return whole if len(parts) == 1 else whole + plus_turned(mm(parts[0], parts[1], NT))
+    if len(parts) == 1:
+        return mm(parts[0], parts[0], NT)
+    high, low = parts
+    return plus_turned(mm(cat([high, high], 1), cat([high * 0.5, low], 1), NT))
 
 
 def square_of(parts):
-    whole = mm(parts[0], parts[0])
-    return whole if len(parts) == 1 else whole + plus_turned(mm(parts[0], parts[1]))
+    if len(parts) == 1:
+        return mm(parts[0], parts[0])
+    high, low = parts
+    return plus_turned(mm(cat([high, high], 1), cat([high * 0.5, low], 0)))
 
 
 def product_of(left, right):

time: 87.8 us -> 88.5 us (level)
  transfers between devices with their start and end apart: 17 -> 17, of which waited for: 9 -> 8; matrix products, arithmetic and copies ran while one was open for 0% -> 0% of each run, Pallas kernels for 37% -> 38%
where the time goes in v4:
time: 88.5 us; the launch traced here: 88.2 us
  Pallas kernels  36.3 us (41%)
  waiting for transfers between devices  28.6 us (32%)
  starting transfers between devices  18.6 us (21%)
  local copies, waits for them, and re-layouts  4.34 us (5%)
    pallas_call x21, Pallas kernels, call(): pl.pallas_call(reading, out_shape=out_shape, in_specs=[VMEM] * count + [A...  34.2 us
    ppermute x17, waiting for transfers between devices, shifted(): return lax.ppermute(value, axis, [(at, at ^ step) for at in range(count)])  28.6 us
    ppermute x17, starting transfers between devices, shifted(): return lax.ppermute(value, axis, [(at, at ^ step) for at in range(count)])  18.6 us
    unnamed x20, local copies, waits for them, and re-layouts  4.34 us
    pallas_call x1, Pallas kernels, first_message(): pl.pallas_call(functools.partial(message_kernel, 0), out_shape=shape(dims...  2.01 us
  transfers between devices with their start and end apart: 17, of which 8 were waited for; matrix products, arithmetic and copies ran while one was open for 0% of the time, Pallas kernels for 38%

profile of v4, /device:TPU:8, one launch (start us, length us, event | category | flops | bytes accessed | tf_op | source)
XLA Modules:
  0.0 88.2 jit_solution(7016717842185479109)
XLA Ops:
  0.0 2.0 %message.2.refs_0_ = bf16[1040,256]{1,0:T(8,128)(2,1)} custom-call(bf16[2,512,256]{2,1,0:T(8,128)(2,1)} %refs_9_.3, bf16[2,512,256]{2,1,0:T(8,128)(2,1)} %refs_10_.3, f32[1,2,512]{2,1,0:T(2,128)} %refs_2_.3), custom_call_target="tpu_custom_call" | custom-call | tf_op jit(solution)/shard_map/message/pallas_call | solution.py:440
  2.0 1.5 %collective-permute-start.1 = (bf16[1040,256]{1,0:T(8,128)(2,1)}, bf16[1040,256]{1,0:T(8,128)(2,1)S(1)}, u32[]{:S(2)}, u32[]{:S(2)}) collective-permute-start(bf16[1040,256]{1,0:T(8,128)(2,1)} %message.2.refs_0_), channel_id=1, source_target_pairs={{0,16},{8,24},{16,0},{24,8},{1,17},{9,25},{17,1},{25,9},{2,18},{10... | collective-permute-start | bytes 1597448 | tf_op jit(solution)/shard_map/ppermute | solution.py:462
  3.5 1.5 %collective-permute-start = (bf16[1040,256]{1,0:T(8,128)(2,1)}, bf16[1040,256]{1,0:T(8,128)(2,1)S(1)}, u32[]{:S(2)}, u32[]{:S(2)}) collective-permute-start(bf16[1040,256]{1,0:T(8,128)(2,1)} %message.2.refs_0_), channel_id=1, source_target_pairs={{0,8},{8,0},{16,24},{24,16},{1,9},{9,1},{17,25},{25,17},{2,10},{10... | collective-permute-start | bytes 1597448 | tf_op jit(solution)/shard_map/ppermute | solution.py:462
  8.2 1.9 %grads.6 = (f32[3,256,512]{2,1,0:T(8,128)S(1)}, bf16[512,1024]{1,0:T(8,128)(2,1)S(1)}, bf16[512,512]{1,0:T(8,128)(2,1)S(1)}) custom-call(bf16[1040,256]{1,0:T(8,128)(2,1)S(1)} %copy-done.2, f32[256,512]{1,0:T(8,128)S(1)} %bitcast.3, f32[256,512]{1,0:T(8,128)S(1)} %bitcast.4, f32[512,256]{1,0:T(8,128)S(1)} %bitcast.5), custom_call_target="tpu_custom_call" | custom-call | tf_op jit(solution)/shard_map/grads/pallas_call | solution.py:420
  12.3 3.8 %collective-permute-done.1.refs_1_.refs_0_ = bf16[1040,256]{1,0:T(8,128)(2,1)S(1)} collective-permute-done((bf16[1040,256]{1,0:T(8,128)(2,1)}, bf16[1040,256]{1,0:T(8,128)(2,1)S(1)}, u32[]{:S(2)}, u32[]{:S(2)}) %collective-permute-start.1) | collective-permute-done | bytes 532512 | tf_op jit(solution)/shard_map/ppermute | solution.py:462
  16.1 1.6 %collective-permute-start.5 = (bf16[528,256]{1,0:T(8,128)(2,1)S(1)}, bf16[528,256]{1,0:T(8,128)(2,1)S(1)}, u32[]{:S(2)}, u32[]{:S(2)}) collective-permute-start(bf16[528,256]{1,0:T(8,128)(2,1)S(1)} %relay.4.refs_1_), channel_id=1, source_target_pairs={{0,8},{8,0},{16,24},{24,16},{1,9},{9,1},{17,25},{25,17},{2,10},{10... | collective-permute-start | bytes 811016 | tf_op jit(solution)/shard_map/ppermute | solution.py:462
  17.7 1.6 %collective-permute-start.4 = (bf16[512,256]{1,0:T(8,128)(2,1)S(1)}, bf16[512,256]{1,0:T(8,128)(2,1)S(1)}, u32[]{:S(2)}, u32[]{:S(2)}) collective-permute-start(bf16[512,256]{1,0:T(8,128)(2,1)S(1)} %relay.5), channel_id=1, source_target_pairs={{0,16},{8,24},{16,0},{24,8},{1,17},{9,25},{17,1},{25,9},{2,18},{10... | collective-permute-start | bytes 786440 | tf_op jit(solution)/shard_map/ppermute | solution.py:462
  19.3 3.4 %grads.7.refs_3_.refs_4_ = f32[3,256,512]{2,1,0:T(8,128)S(1)} custom-call(bf16[1040,256]{1,0:T(8,128)(2,1)S(1)} %collective-permute-done.refs_0_, bf16[1040,256]{1,0:T(8,128)(2,1)S(1)} %collective-permute-done.1.refs_1_.refs_0_, bf16[512,1024]{1,0:T(8,128)(2,1)S(1)} %get-tuple-element.25.refs_2_.refs_5_, ...), custom_call_target="tpu_custom_call" | custom-call | tf_op jit(solution)/shard_map/grads/pallas_call | solution.py:420
  23.3 1.2 %collective-permute-start.2 = (bf16[1040,256]{1,0:T(8,128)(2,1)S(1)}, bf16[1040,256]{1,0:T(8,128)(2,1)S(1)}, u32[]{:S(2)}, u32[]{:S(2)}) collective-permute-start(bf16[1040,256]{1,0:T(8,128)(2,1)S(1)} %message.3.refs_5_.refs_0_), channel_id=1, source_target_pairs={{0,8},{8,0},{16,24},{24,16},{1,9},{9,1},{17,25},{25,17},{2,10},{10... | collective-permute-start | bytes 1597448 | tf_op jit(solution)/shard_map/ppermute | solution.py:462
  24.6 1.8 %grads.8.refs_7_.refs_13_ = f32[3,256,512]{2,1,0:T(8,128)S(1)} custom-call(bf16[512,256]{1,0:T(8,128)(2,1)S(1)} %collective-permute-done.4.refs_0_.refs_1_.refs_3_, bf16[528,256]{1,0:T(8,128)(2,1)S(1)} %collective-permute-done.5.refs_1_.refs_2_.refs_4_, bf16[512,1024]{1,0:T(8,128)(2,1)S(1)} %get-tuple-element.25.refs_2_.refs_5_, ...), custom_call_target="tpu_custom_call" | custom-call | tf_op jit(solution)/shard_map/grads/pallas_call | solution.py:420
  26.4 8.3 %update.2 = (bf16[512,256]{1,0:T(8,128)(2,1)S(1)}, bf16[512,1024]{1,0:T(8,128)(2,1)S(1)}, bf16[512,512]{1,0:T(8,128)(2,1)S(1)}) custom-call(bf16[1040,256]{1,0:T(8,128)(2,1)S(1)} %collective-permute-done.refs_0_, bf16[512,256]{1,0:T(8,128)(2,1)S(1)} %collective-permute-done.4.refs_0_.refs_1_.refs_3_, ...), custom_call_target="tpu_custom_call" | custom-call | flops 30000001024 | tf_op jit(solution)/shard_map/update/pallas_call | solution.py:420
  34.7 1.8 %grads.9.refs_4_ = f32[3,256,512]{2,1,0:T(8,128)S(1)} custom-call(bf16[1040,256]{1,0:T(8,128)(2,1)S(1)} %message.3.refs_5_.refs_0_, bf16[512,1024]{1,0:T(8,128)(2,1)S(1)} %get-tuple-element.31.refs_1_.refs_2_.refs_5_, bf16[512,512]{1,0:T(8,128)(2,1)S(1)} %get-tuple-element.32.refs_2_.refs_3_.refs_6_, bf16[512,256]{1,0:T(8,128)(2,1)S(1)} %get-tuple-element.29.refs_3_.refs_0_), custom_call_target="tpu_custom_call" | custom-call | tf_op jit(solution)/shard_map/grads/pallas_call | solution.py:420
  37.4 1.2 %collective-permute-start.9 = (bf16[528,256]{1,0:T(8,128)(2,1)S(1)}, bf16[528,256]{1,0:T(8,128)(2,1)S(1)}, u32[]{:S(2)}, u32[]{:S(2)}) collective-permute-start(bf16[528,256]{1,0:T(8,128)(2,1)S(1)} %relay.6.refs_1_), channel_id=1, source_target_pairs={{0,8},{8,0},{16,24},{24,16},{1,9},{9,1},{17,25},{25,17},{2,10},{10... | collective-permute-start | bytes 811016 | tf_op jit(solution)/shard_map/ppermute | solution.py:462
  38.6 1.2 %collective-permute-start.8 = (bf16[512,256]{1,0:T(8,128)(2,1)S(1)}, bf16[512,256]{1,0:T(8,128)(2,1)S(1)}, u32[]{:S(2)}, u32[]{:S(2)}) collective-permute-start(bf16[512,256]{1,0:T(8,128)(2,1)S(1)} %relay.7), channel_id=1, source_target_pairs={{0,16},{8,24},{16,0},{24,8},{1,17},{9,25},{17,1},{25,9},{2,18},{10... | collective-permute-start | bytes 786440 | tf_op jit(solution)/shard_map/ppermute | solution.py:462
  40.2 1.6 %collective-permute-start.15 = (bf16[512,256]{1,0:T(8,128)(2,1)S(1)}, bf16[512,256]{1,0:T(8,128)(2,1)S(1)}, u32[]{:S(2)}, u32[]{:S(2)}) collective-permute-start(bf16[512,256]{1,0:T(8,128)(2,1)S(1)} %get-tuple-element.44), channel_id=1, source_target_pairs={{0,2},{1,3},{2,0},{3,1},{4,6},{5,7},{6,4},{7,5},{8,10},{9,11},{10,... | collective-permute-start | bytes 786440 | tf_op jit(solution)/shard_map/ppermute | solution.py:462
  41.8 3.4 %grads.10.refs_4_ = f32[3,256,512]{2,1,0:T(8,128)S(1)} custom-call(bf16[1040,256]{1,0:T(8,128)(2,1)S(1)} %collective-permute-done.2.refs_0_, bf16[1040,256]{1,0:T(8,128)(2,1)S(1)} %collective-permute-done.3.refs_0_.refs_1_, bf16[512,1024]{1,0:T(8,128)(2,1)S(1)} %get-tuple-element.31.refs_1_.refs_2_.refs_5_, ...), custom_call_target="tpu_custom_call" | custom-call | tf_op jit(solution)/shard_map/grads/pallas_call | solution.py:420
  45.1 1.9 %collective-permute-done.8.refs_0_.refs_1_ = bf16[512,256]{1,0:T(8,128)(2,1)S(1)} collective-permute-done((bf16[512,256]{1,0:T(8,128)(2,1)S(1)}, bf16[512,256]{1,0:T(8,128)(2,1)S(1)}, u32[]{:S(2)}, u32[]{:S(2)}) %collective-permute-start.8) | collective-permute-done | bytes 262176 | tf_op jit(solution)/shard_map/ppermute | solution.py:462
  47.1 1.7 %grads.11.refs_2_.refs_7_ = f32[3,256,512]{2,1,0:T(8,128)S(1)} custom-call(bf16[512,256]{1,0:T(8,128)(2,1)S(1)} %collective-permute-done.8.refs_0_.refs_1_, bf16[528,256]{1,0:T(8,128)(2,1)S(1)} %collective-permute-done.9.refs_1_.refs_2_, bf16[512,1024]{1,0:T(8,128)(2,1)S(1)} %get-tuple-element.31.refs_1_.refs_2_.refs_5_, ...), custom_call_target="tpu_custom_call" | custom-call | tf_op jit(solution)/shard_map/grads/pallas_call | solution.py:420
  49.0 2.7 %collective-permute-start.16 = (bf16[512,256]{1,0:T(8,128)(2,1)S(1)}, bf16[512,256]{1,0:T(8,128)(2,1)S(1)}, u32[]{:S(2)}, u32[]{:S(2)}) collective-permute-start(bf16[512,256]{1,0:T(8,128)(2,1)S(1)} %add.1.refs_13_), channel_id=1, source_target_pairs={{0,4},{1,5},{2,6},{3,7},{4,0},{5,1},{6,2},{7,3},{8,12},{9,13},{10,... | collective-permute-start | bytes 786440 | tf_op jit(solution)/shard_map/ppermute | solution.py:462
  51.6 8.3 %update.3.refs_0_ = bf16[512,256]{1,0:T(8,128)(2,1)S(1)} custom-call(bf16[1040,256]{1,0:T(8,128)(2,1)S(1)} %collective-permute-done.2.refs_0_, bf16[512,256]{1,0:T(8,128)(2,1)S(1)} %collective-permute-done.8.refs_0_.refs_1_, bf16[528,256]{1,0:T(8,128)(2,1)S(1)} %collective-permute-done.9.refs_1_.refs_2_, ...), custom_call_target="tpu_custom_call" | custom-call | tf_op jit(solution)/shard_map/update/pallas_call | solution.py:420
  62.9 2.7 %collective-permute-start.14 = (bf16[512,256]{1,0:T(8,128)(2,1)S(1)}, bf16[512,256]{1,0:T(8,128)(2,1)S(1)}, u32[]{:S(2)}, u32[]{:S(2)}) collective-permute-start(bf16[512,256]{1,0:T(8,128)(2,1)S(1)} %get-tuple-element.43), channel_id=1, source_target_pairs={{0,6},{1,7},{2,4},{3,5},{4,2},{5,3},{6,0},{7,1},{8,14},{9,15},{10,... | collective-permute-start | bytes 786440 | tf_op jit(solution)/shard_map/ppermute | solution.py:462
  65.7 8.8 %collective-permute-done.12.refs_1_ = bf16[512,256]{1,0:T(8,128)(2,1)S(1)} collective-permute-done((bf16[512,256]{1,0:T(8,128)(2,1)S(1)}, bf16[512,256]{1,0:T(8,128)(2,1)S(1)}, u32[]{:S(2)}, u32[]{:S(2)}) %collective-permute-start.12) | collective-permute-done | bytes 262176 | tf_op jit(solution)/shard_map/ppermute | solution.py:462
  74.5 1.2 %collective-permute-done.13.refs_2_ = bf16[512,256]{1,0:T(8,128)(2,1)S(1)} collective-permute-done((bf16[512,256]{1,0:T(8,128)(2,1)S(1)}, bf16[512,256]{1,0:T(8,128)(2,1)S(1)}, u32[]{:S(2)}, u32[]{:S(2)}) %collective-permute-start.13) | collective-permute-done | bytes 262176 | tf_op jit(solution)/shard_map/ppermute | solution.py:462
  75.7 11.6 %collective-permute-done.14.refs_3_ = bf16[512,256]{1,0:T(8,128)(2,1)S(1)} collective-permute-done((bf16[512,256]{1,0:T(8,128)(2,1)S(1)}, bf16[512,256]{1,0:T(8,128)(2,1)S(1)}, u32[]{:S(2)}, u32[]{:S(2)}) %collective-permute-start.14) | collective-permute-done | bytes 262176 | tf_op jit(solution)/shard_map/ppermute | solution.py:462
  (52 shorter events, 11.5 us)
Async XLA Ops:
  0.0 5.0 %copy-start.5 = (f32[1,256,512]{2,1,0:T(8,128)S(1)}, f32[1,256,512]{2,1,0:T(8,128)}, u32[]{:S(2)}) copy-start(f32[1,256,512]{2,1,0:T(8,128)} %param.13) | copy-start | bytes 1572868
  0.0 10.1 %copy-start.4 = (bf16[256,2048]{1,0:T(8,128)(2,1)S(1)}, bf16[256,2048]{1,0:T(8,128)(2,1)}, u32[]{:S(2)}) copy-start(bf16[256,2048]{1,0:T(8,128)(2,1)} %refs_0_.3) | copy-start | bytes 3145732
  2.0 14.0 %collective-permute-start.1 = (bf16[1040,256]{1,0:T(8,128)(2,1)}, bf16[1040,256]{1,0:T(8,128)(2,1)S(1)}, u32[]{:S(2)}, u32[]{:S(2)}) collective-permute-start(bf16[1040,256]{1,0:T(8,128)(2,1)} %message.2.refs_0_), channel_id=1, source_target_pairs={{0,16},{8,24},{16,0},{24,8},{1,17},{9,25},{17,1},{25,9},{2,18},{10... | collective-permute-start | bytes 1597448 | tf_op jit(solution)/shard_map/ppermute | solution.py:462
  3.5 14.1 %collective-permute-start = (bf16[1040,256]{1,0:T(8,128)(2,1)}, bf16[1040,256]{1,0:T(8,128)(2,1)S(1)}, u32[]{:S(2)}, u32[]{:S(2)}) collective-permute-start(bf16[1040,256]{1,0:T(8,128)(2,1)} %message.2.refs_0_), channel_id=1, source_target_pairs={{0,8},{8,0},{16,24},{24,16},{1,9},{9,1},{17,25},{25,17},{2,10},{10... | collective-permute-start | bytes 1597448 | tf_op jit(solution)/shard_map/ppermute | solution.py:462
  5.0 1.1 %copy-start.2 = (bf16[1040,256]{1,0:T(8,128)(2,1)S(1)}, bf16[1040,256]{1,0:T(8,128)(2,1)}, u32[]{:S(2)}) copy-start(bf16[1040,256]{1,0:T(8,128)(2,1)} %message.2.refs_0_) | copy-start | bytes 1597444
  10.1 1.2 %copy-start.1 = (bf16[2,512,256]{2,1,0:T(8,128)(2,1)S(1)}, bf16[2,512,256]{2,1,0:T(8,128)(2,1)}, u32[]{:S(2)}) copy-start(bf16[2,512,256]{2,1,0:T(8,128)(2,1)} %refs_10_.3) | copy-start | bytes 1572868
  10.1 1.3 %copy-start.3 = (bf16[2,512,256]{2,1,0:T(8,128)(2,1)S(1)}, bf16[2,512,256]{2,1,0:T(8,128)(2,1)}, u32[]{:S(2)}) copy-start(bf16[2,512,256]{2,1,0:T(8,128)(2,1)} %refs_8_.3) | copy-start | bytes 1572868
  16.1 8.5 %collective-permute-start.5 = (bf16[528,256]{1,0:T(8,128)(2,1)S(1)}, bf16[528,256]{1,0:T(8,128)(2,1)S(1)}, u32[]{:S(2)}, u32[]{:S(2)}) collective-permute-start(bf16[528,256]{1,0:T(8,128)(2,1)S(1)} %relay.4.refs_1_), channel_id=1, source_target_pairs={{0,8},{8,0},{16,24},{24,16},{1,9},{9,1},{17,25},{25,17},{2,10},{10... | collective-permute-start | bytes 811016 | tf_op jit(solution)/shard_map/ppermute | solution.py:462
  17.7 7.0 %collective-permute-start.4 = (bf16[512,256]{1,0:T(8,128)(2,1)S(1)}, bf16[512,256]{1,0:T(8,128)(2,1)S(1)}, u32[]{:S(2)}, u32[]{:S(2)}) collective-permute-start(bf16[512,256]{1,0:T(8,128)(2,1)S(1)} %relay.5), channel_id=1, source_target_pairs={{0,16},{8,24},{16,0},{24,8},{1,17},{9,25},{17,1},{25,9},{2,18},{10... | collective-permute-start | bytes 786440 | tf_op jit(solution)/shard_map/ppermute | solution.py:462
  19.3 17.3 %collective-permute-start.7 = (bf16[256,1024]{1,0:T(8,128)(2,1)S(1)}, bf16[256,1024]{1,0:T(8,128)(2,1)S(1)}, u32[]{:S(2)}, u32[]{:S(2)}) collective-permute-start(bf16[256,1024]{1,0:T(8,128)(2,1)S(1)} %get-tuple-element.30), channel_id=1, source_target_pairs={{0,1},{1,0},{2,3},{3,2},{4,5},{5,4},{6,7},{7,6},{8,9},{9,8},{10,11... | collective-permute-start | bytes 1572872 | tf_op jit(solution)/shard_map/ppermute | solution.py:462
  19.3 3.4 %copy-start.8 = (f32[1,2,512]{2,1,0:T(2,128)S(1)}, f32[1,2,512]{2,1,0:T(2,128)}, u32[]{:S(2)}) copy-start(f32[1,2,512]{2,1,0:T(2,128)} %refs_2_.3) | copy-start | bytes 12292
  22.7 3.7 %copy-start.9 = (f32[1,256]{1,0:T(1,128)S(1)}, f32[1,256]{1,0:T(1,128)}, u32[]{:S(2)}) copy-start(f32[1,256]{1,0:T(1,128)} %refs_12_.3) | copy-start | bytes 3076
  22.7 14.6 %collective-permute-start.3 = (bf16[1040,256]{1,0:T(8,128)(2,1)S(1)}, bf16[1040,256]{1,0:T(8,128)(2,1)S(1)}, u32[]{:S(2)}, u32[]{:S(2)}) collective-permute-start(bf16[1040,256]{1,0:T(8,128)(2,1)S(1)} %message.3.refs_5_.refs_0_), channel_id=1, source_target_pairs={{0,16},{8,24},{16,0},{24,8},{1,17},{9,25},{17,1},{25,9},{2,18},{10... | collective-permute-start | bytes 1597448 | tf_op jit(solution)/shard_map/ppermute | solution.py:462
  23.3 15.3 %collective-permute-start.2 = (bf16[1040,256]{1,0:T(8,128)(2,1)S(1)}, bf16[1040,256]{1,0:T(8,128)(2,1)S(1)}, u32[]{:S(2)}, u32[]{:S(2)}) collective-permute-start(bf16[1040,256]{1,0:T(8,128)(2,1)S(1)} %message.3.refs_5_.refs_0_), channel_id=1, source_target_pairs={{0,8},{8,0},{16,24},{24,16},{1,9},{9,1},{17,25},{25,17},{2,10},{10... | collective-permute-start | bytes 1597448 | tf_op jit(solution)/shard_map/ppermute | solution.py:462
  34.7 1.9 %collective-permute-start.6 = (bf16[512,256]{1,0:T(8,128)(2,1)S(1)}, bf16[512,256]{1,0:T(8,128)(2,1)S(1)}, u32[]{:S(2)}, u32[]{:S(2)}) collective-permute-start(bf16[512,256]{1,0:T(8,128)(2,1)S(1)} %get-tuple-element.29.refs_3_.refs_0_), channel_id=1, source_target_pairs={{0,1},{1,0},{2,3},{3,2},{4,5},{5,4},{6,7},{7,6},{8,9},{9,8},{10,11... | collective-permute-start | bytes 786440 | tf_op jit(solution)/shard_map/ppermute | solution.py:462
  37.4 9.7 %collective-permute-start.9 = (bf16[528,256]{1,0:T(8,128)(2,1)S(1)}, bf16[528,256]{1,0:T(8,128)(2,1)S(1)}, u32[]{:S(2)}, u32[]{:S(2)}) collective-permute-start(bf16[528,256]{1,0:T(8,128)(2,1)S(1)} %relay.6.refs_1_), channel_id=1, source_target_pairs={{0,8},{8,0},{16,24},{24,16},{1,9},{9,1},{17,25},{25,17},{2,10},{10... | collective-permute-start | bytes 811016 | tf_op jit(solution)/shard_map/ppermute | solution.py:462
  38.6 8.5 %collective-permute-start.8 = (bf16[512,256]{1,0:T(8,128)(2,1)S(1)}, bf16[512,256]{1,0:T(8,128)(2,1)S(1)}, u32[]{:S(2)}, u32[]{:S(2)}) collective-permute-start(bf16[512,256]{1,0:T(8,128)(2,1)S(1)} %relay.7), channel_id=1, source_target_pairs={{0,16},{8,24},{16,0},{24,8},{1,17},{9,25},{17,1},{25,9},{2,18},{10... | collective-permute-start | bytes 786440 | tf_op jit(solution)/shard_map/ppermute | solution.py:462
  39.7 9.2 %collective-permute-start.10 = (bf16[512,256]{1,0:T(8,128)(2,1)S(1)}, bf16[512,256]{1,0:T(8,128)(2,1)S(1)}, u32[]{:S(2)}, u32[]{:S(2)}) collective-permute-start(bf16[512,256]{1,0:T(8,128)(2,1)S(1)} %get-tuple-element.35), channel_id=1, source_target_pairs={{0,2},{1,3},{2,0},{3,1},{4,6},{5,7},{6,4},{7,5},{8,10},{9,11},{10,... | collective-permute-start | bytes 786440 | tf_op jit(solution)/shard_map/ppermute | solution.py:462
  40.2 25.4 %collective-permute-start.15 = (bf16[512,256]{1,0:T(8,128)(2,1)S(1)}, bf16[512,256]{1,0:T(8,128)(2,1)S(1)}, u32[]{:S(2)}, u32[]{:S(2)}) collective-permute-start(bf16[512,256]{1,0:T(8,128)(2,1)S(1)} %get-tuple-element.44), channel_id=1, source_target_pairs={{0,2},{1,3},{2,0},{3,1},{4,6},{5,7},{6,4},{7,5},{8,10},{9,11},{10,... | collective-permute-start | bytes 786440 | tf_op jit(solution)/shard_map/ppermute | solution.py:462
  49.0 16.6 %collective-permute-start.16 = (bf16[512,256]{1,0:T(8,128)(2,1)S(1)}, bf16[512,256]{1,0:T(8,128)(2,1)S(1)}, u32[]{:S(2)}, u32[]{:S(2)}) collective-permute-start(bf16[512,256]{1,0:T(8,128)(2,1)S(1)} %add.1.refs_13_), channel_id=1, source_target_pairs={{0,4},{1,5},{2,6},{3,7},{4,0},{5,1},{6,2},{7,3},{8,12},{9,13},{10,... | collective-permute-start | bytes 786440 | tf_op jit(solution)/shard_map/ppermute | solution.py:462
  59.9 1.6 %collective-permute-start.11 = (bf16[512,256]{1,0:T(8,128)(2,1)S(1)}, bf16[512,256]{1,0:T(8,128)(2,1)S(1)}, u32[]{:S(2)}, u32[]{:S(2)}) collective-permute-start(bf16[512,256]{1,0:T(8,128)(2,1)S(1)} %update.3.refs_0_), channel_id=1, source_target_pairs={{0,1},{1,0},{2,3},{3,2},{4,5},{5,4},{6,7},{7,6},{8,9},{9,8},{10,11... | collective-permute-start | bytes 786440 | tf_op jit(solution)/shard_map/ppermute | solution.py:462
  62.0 12.5 %collective-permute-start.12 = (bf16[512,256]{1,0:T(8,128)(2,1)S(1)}, bf16[512,256]{1,0:T(8,128)(2,1)S(1)}, u32[]{:S(2)}, u32[]{:S(2)}) collective-permute-start(bf16[512,256]{1,0:T(8,128)(2,1)S(1)} %get-tuple-element.41), channel_id=1, source_target_pairs={{0,4},{1,5},{2,6},{3,7},{4,0},{5,1},{6,2},{7,3},{8,12},{9,13},{10,... | collective-permute-start | bytes 786440 | tf_op jit(solution)/shard_map/ppermute | solution.py:462
  62.4 13.2 %collective-permute-start.13 = (bf16[512,256]{1,0:T(8,128)(2,1)S(1)}, bf16[512,256]{1,0:T(8,128)(2,1)S(1)}, u32[]{:S(2)}, u32[]{:S(2)}) collective-permute-start(bf16[512,256]{1,0:T(8,128)(2,1)S(1)} %get-tuple-element.42), channel_id=1, source_target_pairs={{0,2},{1,3},{2,0},{3,1},{4,6},{5,7},{6,4},{7,5},{8,10},{9,11},{10,... | collective-permute-start | bytes 786440 | tf_op jit(solution)/shard_map/ppermute | solution.py:462
  62.9 24.4 %collective-permute-start.14 = (bf16[512,256]{1,0:T(8,128)(2,1)S(1)}, bf16[512,256]{1,0:T(8,128)(2,1)S(1)}, u32[]{:S(2)}, u32[]{:S(2)}) collective-permute-start(bf16[512,256]{1,0:T(8,128)(2,1)S(1)} %get-tuple-element.43), channel_id=1, source_target_pairs={{0,6},{1,7},{2,4},{3,5},{4,2},{5,3},{6,0},{7,1},{8,14},{9,15},{10,... | collective-permute-start | bytes 786440 | tf_op jit(solution)/shard_map/ppermute | solution.py:462
  (3 other events, 3.1 us)
